TPU v7x, 512 devices: a whole 4x4x16 slice. The times are simulated.
512 devices in a mesh: blk: 32 (over z, x_hi), rep: 8 (over y, core), mp: 2 (over x_lo).
Axes of the slice: x: 4 (x_hi: 2, x_lo: 2; x = x_hi * 2 + x_lo), y: 4, z: 16, core: 2. Of those that a mesh axis runs over, the one named last changes fastest.
Arguments:
- x_in: bfloat16 [10240, 256], P('blk'), may hold values from -6 to 6
- weight: bfloat16 [256, 256], replicated, may hold values from -0.375 to 0.375
- out_grad: bfloat16 [16384, 256], P('blk'), may hold values from -6 to 6
- adj_vals: bfloat16 [32, 32, 10, 128, 128], P('blk', 'rep', 'mp'), may hold values from -0.15625 to 0.15625
- adj_tiles: int32 [32, 32, 10, 2], P('blk', 'rep', 'mp'), may hold values from 0 to 3, as said below
- adj_mask: int32 [32, 32, 10], P('blk', 'rep', 'mp'), may hold values from 0 to 1, as said below
- send_rows: int32 [32, 32, 16], P('blk'), may hold values from 0 to 319, as said below
- send_counts: int32 [32, 32], replicated, may hold values from 0 to 16, as said below
Outputs:
- hidden: bfloat16 [16384, 256], P('blk')
- weight_grad: float32 [256, 256], replicated
- input_grad: float32 [10240, 256], P('blk')
Inputs may be any that keep to these rules, and one draw needn't show every extreme that they name: For input partition i, the entries send_rows[i, c, s] with s < send_counts[i, c] name every local row 0 to 319 exactly once over all c and s; the other entries are 0. `send_counts`: each row sums to 320; in every draw one owner receives 16 rows from every input partition. `adj_tiles`: within one block pair the 10 tile slots name distinct tile positions. `adj_mask`: every tile slot of offset 0 holds a nonzero tile.
All inputs are finite; a program needn't handle non-finite values.
Results may differ from a plain program's by a relative error of at most 0.005.
Values may be sent and summed in bfloat16 or wider, within the bound.
A program may use at most 64 MiB of HBM per device.

v0:
```python
import math

import jax
import jax.numpy as jnp
from jax import lax
from jax.sharding import PartitionSpec as P


def passed_along(shard, axis, by):
    devices = lax.axis_size(axis)
    return lax.ppermute(shard, axis, [(i, (i + by) % devices) for i in range(devices)])


def aggregate(values, coords, tile_mask, block):
    tile_size = values.shape[1]
    tiles_dim = block.shape[0] // tile_size
    pieces = block.reshape(tiles_dim, tile_size, block.shape[1])
    products = jnp.einsum(
        "nij,njf->nif", values, pieces[coords[:, 1]], preferred_element_type=jnp.float32
    )
    rows_iota = lax.broadcasted_iota(jnp.int32, (tiles_dim, 1), 0)
    choose = ((coords[:, 0][None, :] == rows_iota) & (tile_mask[None, :] == 1)).astype(jnp.float32)
    summed = jnp.einsum("tn,nif->tif", choose, products, precision=lax.Precision.HIGHEST)
    return summed.reshape(block.shape)


def spread(values, coords, tile_mask, gradients):
    tile_size = values.shape[1]
    tiles_dim = gradients.shape[0] // tile_size
    pieces = gradients.reshape(tiles_dim, tile_size, gradients.shape[1])
    products = jnp.einsum(
        "nij,nif->njf", values, pieces[coords[:, 0]], preferred_element_type=jnp.float32
    )
    cols_iota = lax.broadcasted_iota(jnp.int32, (tiles_dim, 1), 0)
    choose = ((coords[:, 1][None, :] == cols_iota) & (tile_mask[None, :] == 1)).astype(jnp.float32)
    summed = jnp.einsum("tn,njf->tjf", choose, products, precision=lax.Precision.HIGHEST)
    return summed.reshape(gradients.shape)


def deliver(buffer):
    return lax.all_to_all(buffer, "blk", split_axis=0, concat_axis=0, tiled=True)


def give_back(buffer):
    return lax.all_to_all(buffer, "blk", split_axis=0, concat_axis=0, tiled=True)


def lanes_total(partial_value):
    return lax.psum(partial_value, ("rep", "mp"))


def shards(x_in, weight, out_grad, adj_vals, adj_tiles, adj_mask, send_rows, send_counts):
    blocks = lax.axis_size("blk")
    stop_count = adj_vals.shape[1]
    rows_blk = out_grad.shape[0]
    slot_count = send_rows.shape[2]
    feat_width = x_in.shape[1]
    my_block = lax.axis_index("blk")
    first_offset = lax.axis_index("rep") * stop_count
    slot_ids = lax.broadcasted_iota(jnp.int32, (blocks, slot_count), 1)
    my_rows = send_rows[0]
    sent_counts = lax.dynamic_index_in_dim(send_counts, my_block, 0, keepdims=False)
    held_counts = lax.dynamic_index_in_dim(send_counts, my_block, 1, keepdims=False)
    sent_live = slot_ids < sent_counts[:, None]
    owned_live = (slot_ids < held_counts[:, None]).reshape(rows_blk)
    outgoing = jnp.where(sent_live[:, :, None], x_in[my_rows], jnp.zeros((), jnp.bfloat16))
    partial_value = jnp.zeros((rows_blk, feat_width), jnp.float32)
    current = deliver(jnp.roll(outgoing, first_offset, axis=0)).reshape(rows_blk, feat_width)
    for stop_index in range(stop_count):
        if stop_index > 0:
            current = passed_along(current, "blk", 1)
        partial_value = partial_value + aggregate(
            adj_vals[0, stop_index], adj_tiles[0, stop_index], adj_mask[0, stop_index], current
        )
    preact = lanes_total(
        jnp.dot(partial_value, weight.astype(jnp.float32), precision=lax.Precision.HIGHEST)
    )
    gate_value = jax.nn.sigmoid(preact)
    hidden = jnp.where(owned_live[:, None], preact * gate_value, 0.0).astype(jnp.bfloat16)
    slope = gate_value * (1.0 + preact * (1.0 - gate_value))
    pre_grad = jnp.where(owned_live[:, None], out_grad.astype(jnp.float32) * slope, 0.0).astype(
        jnp.bfloat16
    )
    weight_part = jnp.einsum(
        "rf,rg->fg", partial_value, pre_grad.astype(jnp.float32), precision=lax.Precision.HIGHEST
    )
    weight_grad = lax.psum(weight_part, ("blk", "rep", "mp")) * (1.0 / math.sqrt(rows_blk * blocks))
    agg_grad = jnp.einsum("rg,fg->rf", pre_grad, weight, preferred_element_type=jnp.float32).astype(
        jnp.bfloat16
    )
    owner_sum = jnp.zeros((blocks, slot_count, feat_width), jnp.float32)
    bundle_back = jnp.stack(
        [
            spread(
                adj_vals[0, stop_index], adj_tiles[0, stop_index], adj_mask[0, stop_index], agg_grad
            ).reshape(blocks, slot_count, feat_width)
            for stop_index in range(stop_count)
        ],
        axis=1,
    )
    returned = give_back(bundle_back)
    for stop_index in range(stop_count):
        owner_sum = owner_sum + jnp.roll(
            returned[:, stop_index], -(first_offset + stop_index), axis=0
        )
    masked_sum = jnp.where(sent_live[:, :, None], owner_sum, 0.0).reshape(-1, feat_width)
    local_grad = (
        jnp.zeros((x_in.shape[0], feat_width), jnp.float32).at[my_rows.reshape(-1)].add(masked_sum)
    )
    input_grad = lanes_total(local_grad)
    return (hidden, weight_grad, input_grad)


def solution(mesh):
    placed = (
        P("blk", None),
        P(),
        P("blk", None),
        P("blk", "rep", "mp", None, None),
        P("blk", "rep", "mp", None),
        P("blk", "rep", "mp"),
        P("blk", None, None),
        P(),
    )
    return jax.shard_map(
        shards,
        mesh=mesh,
        in_specs=placed,
        out_specs=(P("blk", None), P(), P("blk", None)),
        check_vma=False,
    )
```

profile of v0, /device:TPU:1, one launch (start us, length us, event | category | flops | bytes accessed | tf_op | source)
XLA Modules:
  0.0 889.3 jit_solution(11016616732413588478)
XLA Ops:
  7.2 0.8 compare_select_fusion
  8.2 0.7 fusion.80
  8.9 2.0 gather_fusion
  11.1 0.9 fusion.8
  12.0 18.5 %all-to-all-start = ((bf16[32,16,256]{2,1,0:T(8,128)(2,1)}), bf16[32,16,256]{2,1,0:T(8,128)(2,1)S(1)}, u32[]{:S(2)}, u32[]{:S(2)}) async-start(bf16[32,16,256]{2,1,0:T(8,128)(2,1)} %fusion.8), calls=%async_computation | async-start | bytes 524288 | tf_op jit(solution)/shard_map/all_to_all | solution.py:41
  30.9 20.4 %all-to-all-done = bf16[32,16,256]{2,1,0:T(8,128)(2,1)S(1)} async-done(((bf16[32,16,256]{2,1,0:T(8,128)(2,1)}), bf16[32,16,256]{2,1,0:T(8,128)(2,1)S(1)}, u32[]{:S(2)}, u32[]{:S(2)}) %all-to-all-start) | async-done | bytes 262176 | tf_op jit(solution)/shard_map/all_to_all | solution.py:41
  51.2 0.6 gather_fusion.1
  51.8 0.3 convolution_bitcast_fusion.7
  52.1 0.5 copy.39
  52.6 3.3 collective-permute-start
  55.9 1.4 fusion.29
  57.3 6.6 collective-permute-done
  63.9 1.5 gather_fusion.2
  65.4 0.3 convolution_bitcast_fusion.6
  65.7 0.5 copy.41
  66.2 1.9 collective-permute-start.1
  68.1 1.7 convolution_add_fusion.2
  69.8 7.3 collective-permute-done.1
  77.1 0.6 gather_fusion.3
  77.7 0.3 convolution_bitcast_fusion.5
  78.0 0.5 copy.43
  78.5 2.1 collective-permute-start.2
  80.6 1.4 convolution_add_fusion.1
  82.0 7.2 collective-permute-done.2
  89.2 0.6 gather_fusion.4
  89.8 0.3 convolution_bitcast_fusion.4
  90.1 0.5 copy.45
  90.6 0.6 convolution_add_fusion
  91.3 1.2 fusion.81
  92.7 130.6 %all-reduce.4.cloned.1.call-done = f32[512,256]{1,0:T(8,128)} async-done(((f32[512,256]{1,0:T(8,128)}), f32[512,256]{1,0:T(8,128)}) %all-reduce.4.cloned.1.call-update) | async-done | bytes 524304 | tf_op jit(solution)/shard_map/psum | solution.py:49
  223.3 2.0 select_convert_fusion
  225.3 0.3 convolution_convert_fusion
  225.6 0.6 gather_fusion.8
  226.2 0.3 convolution_bitcast_fusion
  226.5 0.5 copy.58
  227.0 0.6 fusion.54
  227.6 0.9 copy.59
  228.5 0.6 gather_fusion.7
  229.0 0.3 convolution_bitcast_fusion.1
  229.3 0.5 copy.55
  229.8 0.6 fusion.50
  230.4 0.9 copy.56
  231.3 0.6 gather_fusion.6
  231.9 0.3 convolution_bitcast_fusion.2
  232.2 0.5 copy.52
  232.6 0.6 fusion.46
  233.3 0.9 copy.53
  234.2 0.6 gather_fusion.5
  234.7 0.3 convolution_bitcast_fusion.3
  235.0 0.5 copy.49
  235.5 0.6 fusion.42
  236.3 0.4 copy-done.7
  236.8 1.5 copy.60
  238.3 14.1 %all-to-all-start.1 = ((f32[32,4,16,256]{3,2,1,0:T(8,128)}), f32[32,4,16,256]{3,2,1,0:T(8,128)S(1)}, u32[]{:S(2)}, u32[]{:S(2)}) async-start(f32[32,4,16,256]{3,2,1,0:T(8,128)} %copy.60), calls=%async_computation.1 | async-start | bytes 4194304 | tf_op jit(solution)/shard_map/all_to_all | solution.py:45
  252.6 1.3 fusion.82
  254.0 0.3 all-reduce.8.cloned.1.call-start
  254.2 94.7 %all-to-all-done.1 = f32[32,4,16,256]{3,2,1,0:T(8,128)S(1)} async-done(((f32[32,4,16,256]{3,2,1,0:T(8,128)}), f32[32,4,16,256]{3,2,1,0:T(8,128)S(1)}, u32[]{:S(2)}, u32[]{:S(2)}) %all-to-all-start.1) | async-done | bytes 2097184 | tf_op jit(solution)/shard_map/all_to_all | solution.py:45
  348.9 0.2 slice_bitcast_fusion.3
  349.1 0.6 fusion.2
  349.7 4.0 scatter_custom_fusion
  353.7 394.6 %all-reduce.6.cloned.1.call-done = f32[256,256]{1,0:T(8,128)} async-done(((f32[256,256]{1,0:T(8,128)}), f32[256,256]{1,0:T(8,128)}) %all-reduce.6.cloned.1.call-update) | async-done | bytes 262160 | tf_op jit(solution)/shard_map/psum | solution.py:87
  748.3 1.7 broadcast_multiply_fusion
  750.0 131.1 %all-reduce.8.cloned.1.call-done = f32[320,256]{1,0:T(8,128)} async-done(((f32[320,256]{1,0:T(8,128)}), f32[320,256]{1,0:T(8,128)}) %all-reduce.8.cloned.1.call-update) | async-done | bytes 327696 | tf_op jit(solution)/shard_map/psum | solution.py:49
  881.1 1.7 copy.78
  (58 shorter events, 1.5 us)
Async XLA Ops:
  7.2 1.8 copy-start
  7.2 23.4 %copy-start.11 = (s32[32,32]{1,0:T(8,128)S(1)}, s32[32,32]{1,0:T(8,128)}, u32[]{:S(2)}) copy-start(s32[32,32]{1,0:T(8,128)} %param.17) | copy-start | bytes 12292
  7.2 23.6 %copy-start.12 = (s32[1,4,5,2]{2,3,1,0:T(2,128)S(1)}, s32[1,4,5,2]{2,3,1,0:T(2,128)}, u32[]{:S(2)}) copy-start(s32[1,4,5,2]{2,3,1,0:T(2,128)} %param.14) | copy-start | bytes 484
  7.2 23.6 %copy-start.13 = (s32[1,4,5]{2,1,0:T(4,128)S(1)}, s32[1,4,5]{2,1,0:T(4,128)}, u32[]{:S(2)}) copy-start(s32[1,4,5]{2,1,0:T(4,128)} %param.15) | copy-start | bytes 244
  8.9 42.9 %copy-start.1 = (bf16[1,4,5,128,128]{4,3,2,1,0:T(8,128)(2,1)S(1)}, bf16[1,4,5,128,128]{4,3,2,1,0:T(8,128)(2,1)}, u32[]{:S(2)}) copy-start(bf16[1,4,5,128,128]{4,3,2,1,0:T(8,128)(2,1)} %param.13) | copy-start | bytes 1966084
  12.0 39.2 %all-to-all-start = ((bf16[32,16,256]{2,1,0:T(8,128)(2,1)}), bf16[32,16,256]{2,1,0:T(8,128)(2,1)S(1)}, u32[]{:S(2)}, u32[]{:S(2)}) async-start(bf16[32,16,256]{2,1,0:T(8,128)(2,1)} %fusion.8), calls=%async_computation | async-start | bytes 524288 | tf_op jit(solution)/shard_map/all_to_all | solution.py:41
  30.5 192.8 %all-reduce.4.cloned.1.call-start = ((), (), s32[]{:S(2)}) async-start(), calls=%async_computation.2 | async-start | bytes 1048576 | tf_op jit(solution)/shard_map/psum | solution.py:49
  52.6 11.3 %collective-permute-start = (bf16[512,256]{1,0:T(8,128)(2,1)S(1)}, bf16[512,256]{1,0:T(8,128)(2,1)}, u32[]{:S(2)}, u32[]{:S(2)}) collective-permute-start(bf16[512,256]{1,0:T(8,128)(2,1)S(1)} %bitcast.175), channel_id=1, source_target_pairs={{0,16},{16,32},{32,48},{48,64},{64,80},{80,96},{96,112},{112,128},... | collective-permute-start | bytes 786440 | tf_op jit(solution)/shard_map/ppermute | solution.py:11
  66.2 10.9 %collective-permute-start.1 = (bf16[512,256]{1,0:T(8,128)(2,1)}, bf16[512,256]{1,0:T(8,128)(2,1)S(1)}, u32[]{:S(2)}, u32[]{:S(2)}) collective-permute-start(bf16[512,256]{1,0:T(8,128)(2,1)} %collective-permute-done), channel_id=1, source_target_pairs={{0,16},{16,32},{32,48},{48,64},{64,80},{80,96},{96,112},{112,128},... | collective-permute-start | bytes 786440 | tf_op jit(solution)/shard_map/ppermute | solution.py:11
  78.5 10.7 %collective-permute-start.2 = (bf16[512,256]{1,0:T(8,128)(2,1)S(1)}, bf16[512,256]{1,0:T(8,128)(2,1)S(1)}, u32[]{:S(2)}, u32[]{:S(2)}) collective-permute-start(bf16[512,256]{1,0:T(8,128)(2,1)S(1)} %collective-permute-done.1), channel_id=1, source_target_pairs={{0,16},{16,32},{32,48},{48,64},{64,80},{80,96},{96,112},{112,128},... | collective-permute-start | bytes 786440 | tf_op jit(solution)/shard_map/ppermute | solution.py:11
  82.0 8.5 copy-start.4
  90.1 1.2 copy-start.8
  90.6 132.7 %copy-start.9 = (bf16[512,256]{1,0:T(8,128)(2,1)S(1)}, bf16[512,256]{1,0:T(8,128)(2,1)}, u32[]{:S(2)}) copy-start(bf16[512,256]{1,0:T(8,128)(2,1)} %param.12) | copy-start | bytes 786436
  225.3 0.8 copy-start.2
  235.0 1.2 copy-start.5
  235.0 1.2 copy-start.6
  235.5 1.1 copy-start.7
  238.3 14.1 %copy-start.10 = (s32[1,32,16]{1,2,0:T(8,128)S(1)}, s32[1,32,16]{1,2,0:T(8,128)}, u32[]{:S(2)}) copy-start(s32[1,32,16]{1,2,0:T(8,128)} %param.16) | copy-start | bytes 6148
  238.3 14.3 %copy-start.3 = (bf16[512,256]{1,0:T(8,128)(2,1)S(1)}, bf16[512,256]{1,0:T(8,128)(2,1)}, u32[]{:S(2)}) copy-start(bf16[512,256]{1,0:T(8,128)(2,1)} %copy-done.2) | copy-start | bytes 786436
  238.3 110.6 %all-to-all-start.1 = ((f32[32,4,16,256]{3,2,1,0:T(8,128)}), f32[32,4,16,256]{3,2,1,0:T(8,128)S(1)}, u32[]{:S(2)}, u32[]{:S(2)}) async-start(f32[32,4,16,256]{3,2,1,0:T(8,128)} %copy.60), calls=%async_computation.1 | async-start | bytes 4194304 | tf_op jit(solution)/shard_map/all_to_all | solution.py:45
  252.4 495.9 %all-reduce.6.cloned.1.call-start = ((), (), s32[]{:S(2)}) async-start(), calls=%async_computation.3 | async-start | bytes 524288 | tf_op jit(solution)/shard_map/psum | solution.py:87
  254.0 627.1 %all-reduce.8.cloned.1.call-start = ((), (), s32[]{:S(2)}) async-start(), calls=%async_computation.4 | async-start | bytes 655360 | tf_op jit(solution)/shard_map/psum | solution.py:49
Sparse Core Ops, SparseCore 0:
  92.6 130.6 all-reduce.3
  260.2 488.1 all-reduce.5
  751.8 129.1 all-reduce.7
where the time goes:
time: 890 us; the launch traced here: 889 us
  waiting for transfers between devices  792 us (89%)
  starting transfers between devices  40.2 us (5%)
  local copies, waits for them, and re-layouts  19.2 us (2%)
  between operations  14.4 us (2%)
  matrix products  12.6 us (1%)
  other arithmetic  10.6 us (1%)
    psum x1, waiting for transfers between devices, shards(): lax.psum(weight_part, ('blk', 'rep', 'mp'))  395 us
    psum x2, waiting for transfers between devices, lanes_total(): return lax.psum(partial_value, ('rep', 'mp'))  262 us
    all_to_all x1, waiting for transfers between devices, give_back(): lax.all_to_all(buffer, 'blk', split_axis=0, concat_axis=0, tiled=True)  94.7 us
    ppermute x3, waiting for transfers between devices, passed_along(): lax.ppermute(shard, axis, [(i, (i + by) % devices) for i in range(devices)])  21.1 us
    all_to_all x1, waiting for transfers between devices, deliver(): lax.all_to_all(buffer, 'blk', split_axis=0, concat_axis=0, tiled=True)  20.4 us
    all_to_all x1, starting transfers between devices, deliver(): lax.all_to_all(buffer, 'blk', split_axis=0, concat_axis=0, tiled=True)  18.5 us
  transfers between devices with their start and end apart: 8, of which 8 were waited for; matrix products, arithmetic and copies ran while one was open for 1% of the time, Pallas kernels for 0%

commit v1 on v0

v1 whole, which is shorter than its diff:
```python
import functools
import math

import jax
import jax.numpy as jnp
from jax import lax
from jax.experimental import pallas as pl
from jax.experimental.pallas import tpu as pltpu
from jax.sharding import PartitionSpec as P

MESH = pl.DeviceIdType.MESH
BF = jnp.bfloat16
F32 = jnp.float32


def dot(a, b, dims=((1,), (0,))):
    return lax.dot_general(a, b, (dims, ((), ())), preferred_element_type=F32)


def send(src, dst, ssem, rsem, **where):
    pltpu.make_async_remote_copy(
        src_ref=src,
        dst_ref=dst,
        send_sem=ssem,
        recv_sem=rsem,
        device_id=where,
        device_id_type=MESH,
    ).start()


def drain(ref, sem):
    pltpu.make_async_copy(ref, ref, sem).wait()


def kernel(
    keys_ref,
    x_ref,
    w_ref,
    og_ref,
    rowc_ref,
    rowr_ref,
    live_ref,
    keyv_ref,
    adj_ref,
    hid_ref,
    wg_ref,
    ig_ref,
    v0, v1, v2, v3,
    kpv, kps,
    dense, denset,
    outg, fbuf, zbuf,
    r1s, r1r, agg,
    pg, gb,
    bs, br, pown, qb, ar, gg,
    wprod, wa, war, wb, wbr, wc, wd,
    loc_sem, adj_ss, adj_rs, key_ss, key_rs, key_ls,
    ss, rs,
):
    vall = (v0, v1, v2, v3)
    b = lax.axis_index("blk")
    r = lax.axis_index("rep")
    m = lax.axis_index("mp")
    s = 2 * lax.rem(r, 2)
    k = m * 8 + r
    quad = lax.rem(b, 4)
    F1, Z, R1, R2, ZB, A2, SELF, G, WA, WB, WC, WD = range(12)

    def in_group(d):
        t = lax.rem(r * 2 + m + d, 16)
        return t // 2, lax.rem(t, 2)

    barrier = pltpu.get_barrier_semaphore()

    def greet_blk(d, _):
        pl.semaphore_signal(
            barrier, inc=1, device_id={"blk": lax.rem(b + d, 32)}, device_id_type=MESH
        )
        return 0

    lax.fori_loop(1, 32, greet_blk, 0)

    def greet_group(d, _):
        tr, tm = in_group(d)
        pl.semaphore_signal(barrier, inc=1, device_id={"rep": tr, "mp": tm}, device_id_type=MESH)
        return 0

    lax.fori_loop(1, 16, greet_group, 0)

    for p in range(4):
        j = lax.rem(s + p, 4)
        pltpu.make_async_copy(adj_ref.at[j], vall[p].at[pl.ds(0, 5)], loc_sem.at[p]).start()
        vall[p][10] = jnp.zeros((128, 128), BF)

    pick = (rowc_ref[...] == lax.broadcasted_iota(jnp.int32, (512, 320), 1)).astype(BF)
    half = pl.ds(pl.multiple_of(m * 128, 128), 128)
    picked = dot(pick, x_ref[:, half]).astype(BF).reshape(32, 16, 128)
    outg[pl.ds(1, 32)] = picked
    outg[0] = picked[31]

    pl.semaphore_wait(barrier, 46)

    send(keyv_ref, kpv, key_ss, key_rs, mp=1 - m)

    def deliver(d, _):
        t = lax.rem(b + d, 32)
        c = lax.rem(t - 4 * r - s + 64, 32)
        send(outg.at[pl.ds(c, 2)], fbuf.at[b], ss.at[F1], rs.at[F1], blk=t)
        return 0

    lax.fori_loop(1, 32, deliver, 0)
    for p in range(4):
        j = lax.rem(s + p, 4)
        send(adj_ref.at[j], vall[p].at[pl.ds(5, 5)], adj_ss.at[p], adj_rs.at[p], mp=1 - m)
    c_own = lax.rem(b - 4 * r - s + 64, 32)
    fbuf[b] = outg[pl.ds(c_own, 2)]

    drain(kpv, key_rs)
    to_smem = pltpu.make_async_copy(kpv, kps, key_ls)
    to_smem.start()
    to_smem.wait()

    for p in range(4):
        j = lax.rem(s + p, 4)
        pltpu.make_async_copy(adj_ref.at[j], vall[p].at[pl.ds(0, 5)], loc_sem.at[p]).wait()
        drain(vall[p].at[pl.ds(5, 5)], adj_rs.at[p])
        own = [keys_ref[j, t] for t in range(5)]
        other = [kps[j, t] for t in range(5)]
        for row in range(4):
            for col in range(4):
                at = jnp.int32(10)
                for t in range(5):
                    at = jnp.where(own[t] == row * 4 + col, t, at)
                    at = jnp.where(other[t] == row * 4 + col, 5 + t, at)
                tile = vall[p][at]
                dense[p, row * 128:(row + 1) * 128, col * 128:(col + 1) * 128] = tile
                denset[p, col * 128:(col + 1) * 128, row * 128:(row + 1) * 128] = tile.T

    drain(fbuf.at[pl.ds(0, 31)], rs.at[F1])
    t = lax.rem(b + 2 - 2 * s + 32, 32)
    send(fbuf, zbuf, ss.at[Z], rs.at[Z], blk=t)
    part = dot(dense[0], fbuf[:, 1].reshape(512, 128))
    part += dot(dense[1], fbuf[:, 0].reshape(512, 128))
    drain(zbuf, rs.at[Z])
    part += dot(dense[2], zbuf[:, 1].reshape(512, 128))
    part += dot(dense[3], zbuf[:, 0].reshape(512, 128))

    r1s[...] = part.astype(BF).reshape(8, 64, 128)
    r1r[r] = r1s[r]

    def scatter(d, _):
        t = lax.rem(r + d, 8)
        send(r1s.at[t], r1r.at[r], ss.at[R1], rs.at[R1], rep=t)
        return 0

    lax.fori_loop(1, 8, scatter, 0)
    drain(r1r.at[pl.ds(0, 7)], rs.at[R1])
    total = r1r[0].astype(F32)
    for i in range(1, 8):
        total += r1r[i].astype(F32)
    agg[k] = total.astype(BF)

    def gather(d, _):
        tr, tm = in_group(d)
        send(agg.at[k], agg.at[k], ss.at[R2], rs.at[R2], rep=tr, mp=tm)
        return 0

    lax.fori_loop(1, 16, gather, 0)
    drain(agg.at[pl.ds(0, 15)], rs.at[R2])

    w_half = w_ref[half, :]
    for q in range(4):
        rows = slice(q * 128, (q + 1) * 128)
        a0 = agg[2 * q:2 * q + 2].reshape(128, 128)
        a1 = agg[8 + 2 * q:10 + 2 * q].reshape(128, 128)
        preact = dot(a0, w_ref[0:128, :]) + dot(a1, w_ref[128:256, :])
        live = live_ref[rows, :] > 0
        gate = jax.nn.sigmoid(preact)
        hid_ref[rows, :] = jnp.where(live, preact * gate, 0.0).astype(BF)
        slope = gate * (1.0 + preact * (1.0 - gate))
        pre = jnp.where(live, og_ref[rows, :].astype(F32) * slope, 0.0).astype(BF)
        pg[rows, :] = pre
        gb[rows, :] = dot(pre, w_half, ((1,), (1,))).astype(BF)

    g = gb[...]
    bs[:, 1] = dot(denset[2], g).astype(BF).reshape(32, 16, 128)
    bs[:, 0] = dot(denset[3], g).astype(BF).reshape(32, 16, 128)
    t = lax.rem(b - 2 + 2 * s + 32, 32)
    send(bs, br, ss.at[ZB], rs.at[ZB], blk=t)

    mine = agg[pl.ds(m * 8, 8)].reshape(512, 128)
    wprod[...] = dot(mine, pg[...], ((0,), (0,))).reshape(8, 16, 256)
    w16 = wprod[r]
    for a in range(2):
        for c in range(2):
            wa[2 * a + c] = w16[a * 8:(a + 1) * 8, c * 128:(c + 1) * 128]
    war[quad] = wa[quad]
    for e in range(1, 4):
        q = lax.rem(quad + e, 4)
        send(wa.at[q], war.at[quad], ss.at[WA], rs.at[WA], blk=b - quad + q)

    pown[1] = dot(denset[0], g)
    pown[0] = dot(denset[1], g)

    drain(war.at[pl.ds(0, 3)], rs.at[WA])
    tile = war[0] + war[1] + war[2] + war[3]
    wb[...] = tile
    eighth = b // 4
    wbr[eighth] = tile
    for e in range(1, 8):
        send(wb, wbr.at[eighth], ss.at[WB], rs.at[WB], blk=lax.rem(b + 4 * e, 32))

    drain(br, rs.at[ZB])
    for q in range(2):
        mixed = pown[q] + br[:, q].reshape(512, 128).astype(F32)
        qb[:, q] = mixed.astype(BF).reshape(32, 16, 128)

    for q in range(2):
        c = lax.rem(b - 4 * r - s + (q - 1) + 64, 32)
        home, slot = c // 4, lax.rem(c, 4)

        @pl.when(home == r)
        def _():
            pltpu.make_async_copy(qb.at[b, q], ar.at[slot, 2 * r + q], rs.at[A2]).start()

        @pl.when(home != r)
        def _():
            send(qb.at[b, q], ar.at[slot, 2 * r + q], ss.at[SELF], rs.at[A2], rep=home)

        def back(d, _):
            i = lax.rem(b + d, 32)
            send(qb.at[i, q], ar.at[slot, 2 * r + q], ss.at[A2], rs.at[A2], blk=i, rep=home)
            return 0

        lax.fori_loop(1, 32, back, 0)

    drain(wbr.at[pl.ds(0, 7)], rs.at[WB])
    tile = wbr[0]
    for i in range(1, 8):
        tile += wbr[i]
    wc[quad] = tile
    for e in range(1, 4):
        q = lax.rem(quad + e, 4)
        send(wc.at[quad], wc.at[quad], ss.at[WC], rs.at[WC], blk=b - quad + q)
    drain(wc.at[pl.ds(0, 3)], rs.at[WC])
    wd[k] = wc[...]

    def spread_w(d, _):
        tr, tm = in_group(d)
        send(wd.at[k], wd.at[k], ss.at[WD], rs.at[WD], rep=tr, mp=tm)
        return 0

    lax.fori_loop(1, 16, spread_w, 0)

    drain(ar, rs.at[A2])
    total = ar[:, 0].astype(F32)
    for i in range(1, 16):
        total += ar[:, i].astype(F32)
    gg[k] = total.reshape(64, 128).astype(BF)

    def share(d, _):
        tr, tm = in_group(d)
        send(gg.at[k], gg.at[k], ss.at[G], rs.at[G], rep=tr, mp=tm)
        return 0

    lax.fori_loop(1, 16, share, 0)

    drain(wd.at[pl.ds(0, 15)], rs.at[WD])
    for i in range(16):
        for a in range(2):
            for c in range(2):
                wg_ref[i * 16 + a * 8:i * 16 + a * 8 + 8, c * 128:(c + 1) * 128] = (
                    wd[i, 2 * a + c] * (1.0 / 128.0)
                )

    place = (rowr_ref[...] == lax.broadcasted_iota(jnp.int32, (320, 512), 0)).astype(BF)
    drain(gg.at[pl.ds(0, 15)], rs.at[G])
    for h in range(2):
        ig_ref[:, h * 128:(h + 1) * 128] = dot(place, gg[8 * h:8 * h + 8].reshape(512, 128))

    drain(keyv_ref, key_ss)
    for p in range(4):
        drain(vall[p].at[pl.ds(5, 5)], adj_ss.at[p])
    drain(fbuf.at[pl.ds(0, 31)], ss.at[F1])
    drain(fbuf, ss.at[Z])
    drain(r1r.at[pl.ds(0, 7)], ss.at[R1])
    drain(agg.at[pl.ds(0, 15)], ss.at[R2])
    drain(bs, ss.at[ZB])
    drain(qb.at[pl.ds(0, 31)], ss.at[A2])
    for q in range(2):
        c = lax.rem(b - 4 * r - s + (q - 1) + 64, 32)

        @pl.when(c // 4 != r)
        def _():
            drain(qb.at[b, q], ss.at[SELF])

    drain(gg.at[pl.ds(0, 15)], ss.at[G])
    drain(wa.at[pl.ds(0, 3)], ss.at[WA])
    drain(wbr.at[pl.ds(0, 7)], ss.at[WB])
    drain(wc.at[pl.ds(0, 3)], ss.at[WC])
    drain(wd.at[pl.ds(0, 15)], ss.at[WD])


def shards(x_in, weight, out_grad, adj_vals, adj_tiles, adj_mask, send_rows, send_counts):
    my_block = lax.axis_index("blk")
    slot_ids = lax.broadcasted_iota(jnp.int32, (32, 16), 1)
    sent = lax.dynamic_index_in_dim(send_counts, my_block, 0, keepdims=False)
    held = lax.dynamic_index_in_dim(send_counts, my_block, 1, keepdims=False)
    rows = jnp.where(slot_ids < sent[:, None], send_rows[0], -1).reshape(512)
    live = (slot_ids < held[:, None]).astype(F32).reshape(512, 1)
    keys = jnp.where(adj_mask[0] == 1, adj_tiles[0, :, :, 0] * 4 + adj_tiles[0, :, :, 1], 16)
    keys = jnp.pad(keys, ((0, 4), (0, 123)), constant_values=16)

    vmem = pl.BlockSpec(memory_space=pltpu.VMEM)
    V = pltpu.VMEM
    dma = pltpu.SemaphoreType.DMA
    return tuple(
        pl.pallas_call(
            kernel,
            out_shape=(
                jax.ShapeDtypeStruct((512, 256), BF),
                jax.ShapeDtypeStruct((256, 256), F32),
                jax.ShapeDtypeStruct((320, 256), F32),
            ),
            in_specs=[pl.BlockSpec(memory_space=pltpu.SMEM)]
            + [vmem] * 7
            + [pl.BlockSpec(memory_space=pl.ANY)],
            out_specs=(vmem, vmem, vmem),
            scratch_shapes=[V((11, 128, 128), BF)] * 4
            + [
                V((8, 128), jnp.int32),
                pltpu.SMEM((8, 128), jnp.int32),
                V((4, 512, 512), BF),
                V((4, 512, 512), BF),
                V((33, 16, 128), BF),
                V((32, 2, 16, 128), BF),
                V((32, 2, 16, 128), BF),
                V((8, 64, 128), BF),
                V((8, 64, 128), BF),
                V((16, 64, 128), BF),
                V((512, 256), BF),
                V((512, 128), BF),
                V((32, 2, 16, 128), BF),
                V((32, 2, 16, 128), BF),
                V((2, 512, 128), F32),
                V((32, 2, 16, 128), BF),
                V((4, 16, 16, 128), BF),
                V((16, 64, 128), BF),
                V((8, 16, 256), F32),
                V((4, 8, 128), F32),
                V((4, 8, 128), F32),
                V((8, 128), F32),
                V((8, 8, 128), F32),
                V((4, 8, 128), F32),
                V((16, 4, 8, 128), F32),
                dma((4,)),
                dma((4,)),
                dma((4,)),
                dma,
                dma,
                dma,
                dma((12,)),
                dma((12,)),
            ],
            compiler_params=pltpu.CompilerParams(
                collective_id=0, has_side_effects=True, vmem_limit_bytes=40 * 1024 * 1024
            ),
            name="graph_layer",
        )(
            keys,
            x_in,
            weight,
            out_grad,
            rows.reshape(512, 1),
            rows.reshape(1, 512),
            live,
            keys,
            adj_vals[0],
        )
    )


def solution(mesh):
    placed = (
        P("blk", None),
        P(),
        P("blk", None),
        P("blk", "rep", "mp", None, None),
        P("blk", "rep", "mp", None),
        P("blk", "rep", "mp"),
        P("blk", None, None),
        P(),
    )
    return jax.shard_map(
        shards,
        mesh=mesh,
        in_specs=placed,
        out_specs=(P("blk", None), P(), P("blk", None)),
        check_vma=False,
    )
```

time: 890 us -> 92.5 us (0.10)
  waiting for transfers between devices: 792 us -> 0 us
  Pallas kernels: 0 us -> 85.7 us
  starting transfers between devices: 40.2 us -> 0 us
  between operations: 14.4 us -> 0.75 us
  local copies, waits for them, and re-layouts: 19.2 us -> 5.59 us
  matrix products: 12.6 us -> 0 us
  other arithmetic: 10.6 us -> 0.19 us
    psum x3 -> x0, waiting for transfers between devices: 656 us -> none  [the longest x1 395 us: shards(): lax.psum(weight_part, ('blk', 'rep', 'mp'))]
    all_to_all x2 -> x0, waiting for transfers between devices: 115 us -> none  [the longest x1 94.7 us: give_back(): lax.all_to_all(buffer, 'blk', split_axis=0, concat_axis=0, tiled=True)]
    pallas_call x0 -> x1, Pallas kernels: none -> 85.7 us  [shards(): pl.pallas_call(kernel, out_shape=(jax.ShapeDtypeStruct((512, 256), BF), j...]
    all_to_all x2 -> x0, starting transfers between devices: 32.5 us -> none  [the longest x1 18.5 us: deliver(): lax.all_to_all(buffer, 'blk', split_axis=0, concat_axis=0, tiled=True)]
    ppermute x3 -> x0, waiting for transfers between devices: 21.1 us -> none  [passed_along(): lax.ppermute(shard, axis, [(i, (i + by) % devices) for i in range(devices)])]
    dot_general x19 -> x0, matrix products: 12.6 us -> none  [the longest x4 5.12 us: aggregate(): jnp.einsum('tn,nif->tif', choose, products, precision=lax.Precision.HIGHEST)]
  transfers between devices with their start and end apart: 8 -> 0, of which waited for: 8 -> 0; matrix products, arithmetic and copies ran while one was open for 1% -> 0% of each run, Pallas kernels for 0% -> 0%
where the time goes in v1:
time: 92.5 us; the launch traced here: 92.3 us
  Pallas kernels  85.7 us (93%)
  local copies, waits for them, and re-layouts  5.59 us (6%)
    pallas_call x1, Pallas kernels, shards(): pl.pallas_call(kernel, out_shape=(jax.ShapeDtypeStruct((512, 256), BF), j...  85.7 us
    unnamed x20, local copies, waits for them, and re-layouts  4.71 us

profile of v1, /device:TPU:1, one launch (start us, length us, event | category | flops | bytes accessed | tf_op | source)
XLA Modules:
  0.0 92.3 jit_solution(14406683482087153206)
XLA Ops:
  0.6 0.0 copy-start
  0.6 0.7 copy-done
  1.4 0.0 copy-start.6
  1.4 0.2 dynamic-slice_reduce_fusion
  1.5 0.0 copy-start.7
  1.6 0.5 copy-done.6
  2.0 0.0 copy-start.5
  2.1 0.0 copy-start.1
  2.1 0.2 copy-done.7
  2.2 0.1 iota_compare_fusion.1
  2.3 0.1 lt.59
  2.4 0.1 fusion
  2.5 0.3 copy-done.5
  2.7 0.1 copy.13
  2.8 0.1 squeeze.16
  2.9 0.2 lt.63
  3.1 0.2 squeeze.18
  3.3 0.0 copy-start.3
  3.3 0.0 copy-start.4
  3.3 0.0 copy-start.2
  3.3 0.2 reshape.106.live_ref
  3.5 0.0 copy-done.1
  3.5 0.7 copy-done.3
  4.2 0.1 copy-done.4
  4.3 0.1 copy-done.2
  4.4 85.7 %graph_layer.1 = (bf16[512,256]{1,0:T(8,128)(2,1)S(1)}, f32[256,256]{1,0:T(8,128)S(1)}, f32[320,256]{1,0:T(8,128)S(1)}) custom-call(s32[8,128]{1,0:T(8,128)S(1)} %pad.4.keys_ref.keyv_ref, bf16[320,256]{1,0:T(8,128)(2,1)S(1)} %copy-done.3, bf16[256,256]{1,0:T(8,128)(2,1)S(1)} %copy-done.4, bf16[512,256]{1,0:T(8,128)(2,1)S(1)} %copy-done.2, ...), custom_call_target="tpu_custom_call" | custom-call | tf_op jit(solution)/shard_map/graph_layer/pallas_call | solution.py:317
  90.1 0.7 copy.21
  90.8 0.7 copy.22
  91.5 0.7 copy.23
  (6 shorter events, 0.1 us)
Async XLA Ops:
  0.6 0.7 copy-start
  1.4 0.7 copy-start.6
  1.5 0.7 copy-start.7
  2.0 0.7 copy-start.5
  2.1 1.5 %copy-start.1 = (bf16[1,4,5,128,128]{4,3,2,1,0:T(8,128)(2,1)S(1)}, bf16[1,4,5,128,128]{4,3,2,1,0:T(8,128)(2,1)}, u32[]{:S(2)}) copy-start(bf16[1,4,5,128,128]{4,3,2,1,0:T(8,128)(2,1)} %param.11) | copy-start | bytes 1966084
  3.3 0.9 copy-start.3
  3.3 1.0 %copy-start.4 = (bf16[256,256]{1,0:T(8,128)(2,1)S(1)}, bf16[256,256]{1,0:T(8,128)(2,1)}, u32[]{:S(2)}) copy-start(bf16[256,256]{1,0:T(8,128)(2,1)} %w_ref.1) | copy-start | bytes 393220
  3.3 1.1 %copy-start.2 = (bf16[512,256]{1,0:T(8,128)(2,1)S(1)}, bf16[512,256]{1,0:T(8,128)(2,1)}, u32[]{:S(2)}) copy-start(bf16[512,256]{1,0:T(8,128)(2,1)} %og_ref.1) | copy-start | bytes 786436

commit v2 on v1

v2 whole, which is shorter than its diff:
```python
import functools

import jax
import jax.numpy as jnp
from jax import lax
from jax.experimental import pallas as pl
from jax.experimental.pallas import tpu as pltpu
from jax.sharding import PartitionSpec as P

MESH = pl.DeviceIdType.MESH
BF = jnp.bfloat16
F32 = jnp.float32


def dot(a, b, dims=((1,), (0,))):
    return lax.dot_general(a, b, (dims, ((), ())), preferred_element_type=F32)


def send(src, dst, ssem, rsem, **where):
    pltpu.make_async_remote_copy(
        src_ref=src,
        dst_ref=dst,
        send_sem=ssem,
        recv_sem=rsem,
        device_id=where,
        device_id_type=MESH,
    ).start()


def drain(ref, sem):
    pltpu.make_async_copy(ref, ref, sem).wait()


def both_ways(n):
    d = 16 - (n + 1) // 2
    return jnp.where(lax.rem(n, 2) == 0, d, 32 - d)


def kernel(
    tiles_ref,
    mask_ref,
    x_ref,
    w_ref,
    og_ref,
    rows_ref,
    counts_ref,
    adj_ref,
    hid_ref,
    wg_ref,
    ig_ref,
    v0, v1, v2, v3,
    xv, wv, ogv, rowsv, countsv,
    own_ts, own_ms, mp_tv, mp_mv, mp_ts, mp_ms,
    dense, denset,
    outg, fbuf, zbuf,
    r1s, r1r, agg,
    pg, gb,
    bs, br, qb, ar, gg,
    wprod, wa, war, wb, wbr, wc, wd,
    loc_sem, in_sem, adj_ss, adj_rs, key_ss, key_rs, key_ls,
    ss, rs,
):
    vall = (v0, v1, v2, v3)
    b = lax.axis_index("blk")
    r = lax.axis_index("rep")
    m = lax.axis_index("mp")
    s = 2 * lax.rem(r, 2)
    h = lax.rem(m + b, 2)
    k = h * 8 + r
    quad = lax.rem(b, 4)
    F1, Z, R1, R2, ZB, A2, SELF, G, WA, WB, WC, WD = range(0, 24, 2)

    def at_blk(t):
        return {"blk": t, "mp": lax.rem(h + t, 2)}

    def in_group(d):
        t = lax.rem(r * 2 + m + d, 16)
        return t // 2, lax.rem(t, 2)

    barrier = pltpu.get_barrier_semaphore()

    def greet_blk(d, _):
        pl.semaphore_signal(
            barrier, inc=1, device_id=at_blk(lax.rem(b + d, 32)), device_id_type=MESH
        )
        return 0

    lax.fori_loop(1, 32, greet_blk, 0)

    def greet_group(d, _):
        tr, tm = in_group(d)
        pl.semaphore_signal(barrier, inc=1, device_id={"rep": tr, "mp": tm}, device_id_type=MESH)
        return 0

    lax.fori_loop(1, 16, greet_group, 0)

    staged = (
        (rows_ref, rowsv),
        (counts_ref, countsv),
        (x_ref, xv),
        (tiles_ref, own_ts),
        (mask_ref, own_ms),
        (w_ref, wv),
        (og_ref, ogv),
    )
    for i, (src, dst) in enumerate(staged):
        pltpu.make_async_copy(src, dst, in_sem.at[i]).start()

    def arrived(i):
        src, dst = staged[i]
        pltpu.make_async_copy(src, dst, in_sem.at[i]).wait()

    for p in range(4):
        j = lax.rem(s + p, 4)
        pltpu.make_async_copy(adj_ref.at[j], vall[p].at[pl.ds(0, 5)], loc_sem.at[p]).start()
        vall[p][10] = jnp.zeros((128, 128), BF)

    pl.semaphore_wait(barrier, 46)

    send(tiles_ref, mp_tv, key_ss.at[0], key_rs.at[0], mp=1 - m)
    send(mask_ref, mp_mv, key_ss.at[1], key_rs.at[1], mp=1 - m)

    def pass_tiles(p):
        j = lax.rem(s + p, 4)
        send(adj_ref.at[j], vall[p].at[pl.ds(5, 5)], adj_ss.at[p], adj_rs.at[p], mp=1 - m)

    for p in range(4):
        pass_tiles(p)

    iota = functools.partial(lax.broadcasted_iota, jnp.int32)
    expand = (iota((512, 32), 0) // 16 == iota((512, 32), 1)).astype(BF)
    in_slot = lax.rem(iota((512, 16), 0), 16) == iota((512, 16), 1)
    mine = (iota((32, 16), 0) == b).astype(BF)
    arrived(0)
    arrived(1)
    counts = countsv[...].astype(F32).astype(BF)
    sent = dot(mine, counts, ((0,), (0,)))
    row = jnp.where(iota((16, 32), 0).astype(F32) < sent, rowsv[...], 384)
    high = (row // 128).astype(F32).astype(BF)
    low = lax.rem(row, 128).astype(F32).astype(BF)
    full = dot(expand, high, ((1,), (1,))) * 128.0 + dot(expand, low, ((1,), (1,)))
    rowc = jnp.sum(jnp.where(in_slot, full, 0.0), axis=1, keepdims=True)

    pick = (rowc == iota((512, 320), 1).astype(F32)).astype(BF)
    half = pl.ds(pl.multiple_of(h * 128, 128), 128)
    arrived(2)
    picked = dot(pick, xv[:, half]).astype(BF).reshape(32, 16, 128)
    outg[pl.ds(1, 32)] = picked
    outg[0] = picked[31]

    def deliver(n, _):
        t = lax.rem(b + both_ways(n), 32)
        c = lax.rem(t - 4 * r - s + 64, 32)
        send(outg.at[pl.ds(c, 2)], fbuf.at[b], ss.at[F1], rs.at[F1], **at_blk(t))
        return 0

    lax.fori_loop(0, 31, deliver, 0)
    c_own = lax.rem(b - 4 * r - s + 64, 32)
    fbuf[b] = outg[pl.ds(c_own, 2)]

    held = dot(counts, mine)
    alive = dot(expand, (iota((32, 16), 1).astype(F32) < held).astype(BF))
    live = jnp.sum(jnp.where(in_slot, alive, 0.0), axis=1, keepdims=True) > 0.5
    expand_t = (iota((32, 512), 1) // 16 == iota((32, 512), 0)).astype(BF)
    in_slot_t = lax.rem(iota((16, 512), 1), 16) == iota((16, 512), 0)
    full_t = dot(high, expand_t) * 128.0 + dot(low, expand_t)
    rowr = jnp.sum(jnp.where(in_slot_t, full_t, 0.0), axis=0, keepdims=True)

    arrived(3)
    arrived(4)
    drain(mp_tv, key_rs.at[0])
    drain(mp_mv, key_rs.at[1])
    for i, (src, dst) in enumerate(((mp_tv, mp_ts), (mp_mv, mp_ms))):
        pltpu.make_async_copy(src, dst, key_ls.at[i]).start()
    for i, (src, dst) in enumerate(((mp_tv, mp_ts), (mp_mv, mp_ms))):
        pltpu.make_async_copy(src, dst, key_ls.at[i]).wait()

    def build(p):
        j = lax.rem(s + p, 4)
        pltpu.make_async_copy(adj_ref.at[j], vall[p].at[pl.ds(0, 5)], loc_sem.at[p]).wait()
        drain(vall[p].at[pl.ds(5, 5)], adj_rs.at[p])

        def places(ts, ms):
            return [
                jnp.where(ms[j, t] == 1, ts[j, 0, t] * 4 + ts[j, 1, t], 16) for t in range(5)
            ]

        own, other = places(own_ts, own_ms), places(mp_ts, mp_ms)
        for row in range(4):
            for col in range(4):
                at = jnp.int32(10)
                for t in range(5):
                    at = jnp.where(own[t] == row * 4 + col, t, at)
                    at = jnp.where(other[t] == row * 4 + col, 5 + t, at)
                tile = vall[p][at]
                dense[p, row * 128:(row + 1) * 128, col * 128:(col + 1) * 128] = tile

    def transpose(p):
        for row in range(4):
            for col in range(4):
                tile = dense[p, row * 128:(row + 1) * 128, col * 128:(col + 1) * 128]
                denset[p, col * 128:(col + 1) * 128, row * 128:(row + 1) * 128] = tile.T

    for p in range(3):
        build(p)

    drain(fbuf.at[pl.ds(0, 31)], rs.at[F1])
    t = lax.rem(b + 2 - 2 * s + 32, 32)
    send(fbuf, zbuf, ss.at[Z], rs.at[Z], **at_blk(t))
    part = dot(dense[0], fbuf[:, 1].reshape(512, 128))
    part += dot(dense[1], fbuf[:, 0].reshape(512, 128))
    build(3)
    drain(zbuf, rs.at[Z])
    part += dot(dense[2], zbuf[:, 1].reshape(512, 128))
    part += dot(dense[3], zbuf[:, 0].reshape(512, 128))

    r1s[...] = part.astype(BF).reshape(8, 64, 128)
    r1r[r] = r1s[r]

    def scatter(d, _):
        t = lax.rem(r + d, 8)
        send(r1s.at[t], r1r.at[r], ss.at[R1], rs.at[R1], rep=t)
        return 0

    lax.fori_loop(1, 8, scatter, 0)
    transpose(2)
    transpose(3)
    drain(r1r.at[pl.ds(0, 7)], rs.at[R1])
    total = r1r[0].astype(F32)
    for i in range(1, 8):
        total += r1r[i].astype(F32)
    agg[k] = total.astype(BF)

    def gather(d, _):
        tr, tm = in_group(d)
        send(agg.at[k], agg.at[k], ss.at[R2], rs.at[R2], rep=tr, mp=tm)
        return 0

    lax.fori_loop(1, 16, gather, 0)
    transpose(0)
    transpose(1)
    drain(agg.at[pl.ds(0, 15)], rs.at[R2])

    arrived(5)
    arrived(6)
    w_half = wv[half, :]
    for q in range(4):
        rows = slice(q * 128, (q + 1) * 128)
        a0 = agg[2 * q:2 * q + 2].reshape(128, 128)
        a1 = agg[8 + 2 * q:10 + 2 * q].reshape(128, 128)
        preact = dot(a0, wv[0:128, :]) + dot(a1, wv[128:256, :])
        gate = jax.nn.sigmoid(preact)
        hid_ref[rows, :] = jnp.where(live[rows], preact * gate, 0.0).astype(BF)
        slope = gate * (1.0 + preact * (1.0 - gate))
        pre = jnp.where(live[rows], ogv[rows, :].astype(F32) * slope, 0.0).astype(BF)
        pg[rows, :] = pre
        gb[rows, :] = dot(pre, w_half, ((1,), (1,))).astype(BF)

    g = gb[...]
    t = lax.rem(b - 2 + 2 * s + 32, 32)
    for q in (1, 0):
        bs[q] = dot(denset[3 - q], g).astype(BF)
        send(bs.at[q], br.at[q], ss.at[ZB + q], rs.at[ZB + q], **at_blk(t))

    wprod[...] = dot(agg[pl.ds(h * 8, 8)].reshape(512, 128), pg[...], ((0,), (0,))).reshape(
        8, 16, 256
    )
    w16 = wprod[r]
    for a in range(2):
        for c in range(2):
            wa[2 * a + c] = w16[a * 8:(a + 1) * 8, c * 128:(c + 1) * 128]
    war[quad] = wa[quad]
    for e in range(1, 4):
        q = lax.rem(quad + e, 4)
        send(wa.at[q], war.at[quad], ss.at[WA], rs.at[WA], **at_blk(b - quad + q))
    eighth = b // 4

    for q in (1, 0):
        own = dot(denset[1 - q], g)
        drain(br.at[q], rs.at[ZB + q])
        qb[q] = (own + br[q].astype(F32)).astype(BF).reshape(32, 16, 128)
        if q == 1:
            drain(war.at[pl.ds(0, 3)], rs.at[WA])
            tile = war[0] + war[1] + war[2] + war[3]
            wb[...] = tile
            wbr[eighth] = tile
            for e in range(1, 8):
                send(wb, wbr.at[eighth], ss.at[WB], rs.at[WB], **at_blk(lax.rem(b + 4 * e, 32)))
        c = lax.rem(b - 4 * r - s + (q - 1) + 64, 32)
        home, slot = c // 4, lax.rem(c, 4)

        @pl.when(home == r)
        def _():
            pltpu.make_async_copy(qb.at[q, b], ar.at[slot, 2 * r + q], rs.at[A2]).start()

        @pl.when(home != r)
        def _():
            send(qb.at[q, b], ar.at[slot, 2 * r + q], ss.at[SELF + q], rs.at[A2], rep=home)

        def back(n, _):
            i = lax.rem(b + both_ways(n), 32)
            send(
                qb.at[q, i],
                ar.at[slot, 2 * r + q],
                ss.at[A2 + q],
                rs.at[A2],
                rep=home,
                **at_blk(i),
            )
            return 0

        lax.fori_loop(0, 31, back, 0)

    drain(wbr.at[pl.ds(0, 7)], rs.at[WB])
    tile = wbr[0]
    for i in range(1, 8):
        tile += wbr[i]
    wc[quad] = tile
    for e in range(1, 4):
        q = lax.rem(quad + e, 4)
        send(wc.at[quad], wc.at[quad], ss.at[WC], rs.at[WC], **at_blk(b - quad + q))
    place = (rowr == iota((320, 512), 0).astype(F32)).astype(BF)
    drain(wc.at[pl.ds(0, 3)], rs.at[WC])
    wd[k] = wc[...]

    def spread_w(d, _):
        tr, tm = in_group(d)
        send(wd.at[k], wd.at[k], ss.at[WD], rs.at[WD], rep=tr, mp=tm)
        return 0

    lax.fori_loop(1, 16, spread_w, 0)

    drain(ar, rs.at[A2])
    total = ar[:, 0].astype(F32)
    for i in range(1, 16):
        total += ar[:, i].astype(F32)
    gg[k] = total.reshape(64, 128).astype(BF)

    def share(d, _):
        tr, tm = in_group(d)
        send(gg.at[k], gg.at[k], ss.at[G], rs.at[G], rep=tr, mp=tm)
        return 0

    lax.fori_loop(1, 16, share, 0)

    drain(wd.at[pl.ds(0, 15)], rs.at[WD])
    for i in range(16):
        for a in range(2):
            for c in range(2):
                wg_ref[i * 16 + a * 8:i * 16 + a * 8 + 8, c * 128:(c + 1) * 128] = (
                    wd[i, 2 * a + c] * (1.0 / 128.0)
                )

    drain(gg.at[pl.ds(0, 15)], rs.at[G])
    for h in range(2):
        ig_ref[:, h * 128:(h + 1) * 128] = dot(place, gg[8 * h:8 * h + 8].reshape(512, 128))


    drain(mp_tv, key_ss.at[0])
    drain(mp_mv, key_ss.at[1])
    for p in range(4):
        drain(vall[p].at[pl.ds(5, 5)], adj_ss.at[p])
    drain(fbuf.at[pl.ds(0, 31)], ss.at[F1])
    drain(fbuf, ss.at[Z])
    drain(r1r.at[pl.ds(0, 7)], ss.at[R1])
    drain(agg.at[pl.ds(0, 15)], ss.at[R2])
    for q in range(2):
        drain(bs.at[q], ss.at[ZB + q])
        drain(qb.at[q, pl.ds(0, 31)], ss.at[A2 + q])
        c = lax.rem(b - 4 * r - s + (q - 1) + 64, 32)

        @pl.when(c // 4 != r)
        def _():
            drain(qb.at[q, b], ss.at[SELF + q])

    drain(gg.at[pl.ds(0, 15)], ss.at[G])
    drain(wa.at[pl.ds(0, 3)], ss.at[WA])
    drain(wbr.at[pl.ds(0, 7)], ss.at[WB])
    drain(wc.at[pl.ds(0, 3)], ss.at[WC])
    drain(wd.at[pl.ds(0, 15)], ss.at[WD])


def hand_over(a0, a1, a2, o0, o1, o2, v0, v1, v2, sem):
    trips = ((a0, v0, o0), (a1, v1, o1), (a2, v2, o2))
    for i, (src, mid, _) in enumerate(trips):
        pltpu.make_async_copy(src, mid, sem.at[i]).start()
    for i, (src, mid, dst) in enumerate(trips):
        pltpu.make_async_copy(src, mid, sem.at[i]).wait()
        pltpu.make_async_copy(mid, dst, sem.at[3 + i]).start()
    for i, (_, mid, dst) in enumerate(trips):
        pltpu.make_async_copy(mid, dst, sem.at[3 + i]).wait()


def shards(x_in, weight, out_grad, adj_vals, adj_tiles, adj_mask, send_rows, send_counts):
    hbm = pl.BlockSpec(memory_space=pltpu.HBM)
    vmem = pl.BlockSpec(memory_space=pltpu.VMEM)
    V = pltpu.VMEM
    S = pltpu.SMEM
    I32 = jnp.int32
    dma = pltpu.SemaphoreType.DMA
    outs = (
        jax.ShapeDtypeStruct((512, 256), BF),
        jax.ShapeDtypeStruct((256, 256), F32),
        jax.ShapeDtypeStruct((320, 256), F32),
    )
    results = pl.pallas_call(
        kernel,
        out_shape=outs,
        in_specs=[hbm] * 8,
        out_specs=(vmem,) * 3,
        scratch_shapes=[V((11, 128, 128), BF)] * 4
        + [
            V((320, 256), BF),
            V((256, 256), BF),
            V((512, 256), BF),
            V((16, 32), I32),
            V((32, 32), I32),
            S((4, 2, 5), I32),
            S((4, 5), I32),
            V((4, 2, 5), I32),
            V((4, 5), I32),
            S((4, 2, 5), I32),
            S((4, 5), I32),
            V((4, 512, 512), BF),
            V((4, 512, 512), BF),
            V((33, 16, 128), BF),
            V((32, 2, 16, 128), BF),
            V((32, 2, 16, 128), BF),
            V((8, 64, 128), BF),
            V((8, 64, 128), BF),
            V((16, 64, 128), BF),
            V((512, 256), BF),
            V((512, 128), BF),
            V((2, 512, 128), BF),
            V((2, 512, 128), BF),
            V((2, 32, 16, 128), BF),
            V((4, 16, 16, 128), BF),
            V((16, 64, 128), BF),
            V((8, 16, 256), F32),
            V((4, 8, 128), F32),
            V((4, 8, 128), F32),
            V((8, 128), F32),
            V((8, 8, 128), F32),
            V((4, 8, 128), F32),
            V((16, 4, 8, 128), F32),
            dma((4,)),
            dma((7,)),
            dma((4,)),
            dma((4,)),
            dma((2,)),
            dma((2,)),
            dma((2,)),
            dma((24,)),
            dma((24,)),
        ],
        compiler_params=pltpu.CompilerParams(
            collective_id=0, has_side_effects=True, vmem_limit_bytes=62 * 1024 * 1024
        ),
        name="graph_layer",
    )(
        jnp.swapaxes(adj_tiles[0], 1, 2),
        adj_mask[0],
        x_in,
        weight,
        out_grad,
        send_rows[0].T,
        send_counts,
        adj_vals[0],
    )
    return pl.pallas_call(
        hand_over,
        out_shape=outs,
        in_specs=[pl.BlockSpec(memory_space=pl.ANY)] * 3,
        out_specs=(hbm,) * 3,
        scratch_shapes=[V(o.shape, o.dtype) for o in outs] + [dma((6,))],
        compiler_params=pltpu.CompilerParams(vmem_limit_bytes=62 * 1024 * 1024),
        name="hand_over",
    )(*results)


def solution(mesh):
    placed = (
        P("blk", None),
        P(),
        P("blk", None),
        P("blk", "rep", "mp", None, None),
        P("blk", "rep", "mp", None),
        P("blk", "rep", "mp"),
        P("blk", None, None),
        P(),
    )
    return jax.shard_map(
        shards,
        mesh=mesh,
        in_specs=placed,
        out_specs=(P("blk", None), P(), P("blk", None)),
        check_vma=False,
    )
```

time: 92.5 us -> 82.4 us (0.89)
  local copies, waits for them, and re-layouts: 5.59 us -> 0 us
  Pallas kernels: 85.7 us -> 81.6 us
    unnamed x20 -> x0, local copies, waits for them, and re-layouts: 4.71 us -> none
    pallas_call x1 -> x2, Pallas kernels: 85.7 us -> 81.6 us  [the longest x1 79.7 us: shards(): pl.pallas_call(kernel, out_shape=outs, in_specs=[hbm] * 8, out_specs=(vme...]
where the time goes in v2:
time: 82.4 us; the launch traced here: 82.2 us
  Pallas kernels  81.6 us (99%)
    pallas_call x1, Pallas kernels, shards(): pl.pallas_call(kernel, out_shape=outs, in_specs=[hbm] * 8, out_specs=(vme...  79.7 us
    pallas_call x1, Pallas kernels, shards(): pl.pallas_call(hand_over, out_shape=outs, in_specs=[pl.BlockSpec(memory_s...  1.91 us

profile of v2, /device:TPU:1, one launch (start us, length us, event | category | flops | bytes accessed | tf_op | source)
XLA Modules:
  0.0 82.2 jit_solution(8612235203501395237)
XLA Ops:
  0.6 79.7 %graph_layer.1 = (bf16[512,256]{1,0:T(8,128)(2,1)}, f32[256,256]{1,0:T(8,128)}, f32[320,256]{1,0:T(8,128)}) custom-call(s32[4,2,5]{2,1,0:T(2,128)} %bitcast.10, s32[4,5]{1,0:T(4,128)} %bitcast.11, bf16[320,256]{1,0:T(8,128)(2,1)} %x_ref.1, bf16[256,256]{1,0:T(8,128)(2,1)} %w_ref.1, bf16[512,256]{1,0:T(8,128)(2,1)} %og_ref.1, s32[16,32]{1,0:T(8,128)} %bitcast.9, ...), custom_call_target="tpu_custom_call" | custom-call | tf_op jit(solution)/shard_map/graph_layer/pallas_call | solution.py:406
  80.3 1.9 %hand_over.1 = (bf16[512,256]{1,0:T(8,128)(2,1)}, f32[256,256]{1,0:T(8,128)}, f32[320,256]{1,0:T(8,128)}) custom-call(bf16[512,256]{1,0:T(8,128)(2,1)} %get-tuple-element.6.a0, f32[256,256]{1,0:T(8,128)} %get-tuple-element.7.a1, f32[320,256]{1,0:T(8,128)} %get-tuple-element.8.a2), custom_call_target="tpu_custom_call" | custom-call | tf_op jit(solution)/shard_map/hand_over/pallas_call | solution.py:470

commit v3 on v2

v3 whole, which is shorter than its diff:
```python
import functools

import jax
import jax.numpy as jnp
from jax import lax
from jax.experimental import pallas as pl
from jax.experimental.pallas import tpu as pltpu
from jax.sharding import PartitionSpec as P

MESH = pl.DeviceIdType.MESH
BF = jnp.bfloat16
F32 = jnp.float32


def dot(a, b, dims=((1,), (0,))):
    return lax.dot_general(a, b, (dims, ((), ())), preferred_element_type=F32)


def send(src, dst, ssem, rsem, **where):
    pltpu.make_async_remote_copy(
        src_ref=src,
        dst_ref=dst,
        send_sem=ssem,
        recv_sem=rsem,
        device_id=where,
        device_id_type=MESH,
    ).start()


def drain(ref, sem):
    pltpu.make_async_copy(ref, ref, sem).wait()


def kernel(
    tiles_ref,
    mask_ref,
    x_ref,
    w_ref,
    og_ref,
    rows_ref,
    counts_ref,
    adj_ref,
    hid_ref,
    wg_ref,
    ig_ref,
    v0, v1,
    xv, wv, ogv, rowsv, countsv,
    own_ts, own_ms, mp_tv, mp_mv, mp_ts, mp_ms,
    dense, denset,
    outg, fq, fr, nat,
    r1s, r1r, agg,
    pg, gb,
    pb, xr, mb, ar, gg,
    wprod, wa, war, wb, wbr, wc, wd,
    hidv, wgv, igv,
    loc_sem, in_sem, out_sem, adj_ss, adj_rs, key_ss, key_rs, key_ls,
    ss, rs,
):
    vall = (v0, v1)
    b = lax.axis_index("blk")
    r = lax.axis_index("rep")
    m = lax.axis_index("mp")
    z = b // 2
    parity = lax.rem(b, 2)
    h = lax.rem(m + b, 2)
    k = r * 2 + m
    kw = r * 2 + h
    quad = lax.rem(b, 4)
    R1, R2, G, WA, WB, WC, WD, A2 = range(8)
    F1, XF, XB, A2S, SELF = 8, 10, 12, 14, 16

    def at_blk(t):
        return {"blk": t, "mp": lax.rem(h + t, 2)}

    def in_group(d):
        t = lax.rem(k + d, 16)
        return t // 2, lax.rem(t, 2)

    barrier = pltpu.get_barrier_semaphore()

    def greet(where):
        pl.semaphore_signal(barrier, inc=1, device_id=where, device_id_type=MESH)

    greet({"blk": lax.rem(b + 16, 32)})

    def greet_z(n, _):
        greet({"blk": lax.rem(b + 14 - 2 * n, 32)})
        greet({"blk": lax.rem(b + 18 + 2 * n, 32)})
        return 0

    lax.fori_loop(0, 7, greet_z, 0)

    def greet_group(d, _):
        tr, tm = in_group(d)
        greet({"rep": tr, "mp": tm})
        return 0

    lax.fori_loop(1, 16, greet_group, 0)
    for d in (29, 3, 31, 1):
        greet(at_blk(lax.rem(b + d, 32)))

    staged = (
        (rows_ref, rowsv),
        (counts_ref, countsv),
        (x_ref, xv),
        (tiles_ref, own_ts),
        (mask_ref, own_ms),
        (w_ref, wv),
        (og_ref, ogv),
    )
    for i, (src, dst) in enumerate(staged):
        pltpu.make_async_copy(src, dst, in_sem.at[i]).start()

    def arrived(i):
        src, dst = staged[i]
        pltpu.make_async_copy(src, dst, in_sem.at[i]).wait()

    for p in range(2):
        pltpu.make_async_copy(
            adj_ref.at[m + 2 * p], vall[p].at[pl.ds(0, 5)], loc_sem.at[p]
        ).start()
        vall[p][10] = jnp.zeros((128, 128), BF)

    pl.semaphore_wait(barrier, 34)

    send(tiles_ref, mp_tv, key_ss.at[0], key_rs.at[0], mp=1 - m)
    send(mask_ref, mp_mv, key_ss.at[1], key_rs.at[1], mp=1 - m)
    for p in range(2):
        send(
            adj_ref.at[1 - m + 2 * p],
            vall[p].at[pl.ds(5, 5)],
            adj_ss.at[p],
            adj_rs.at[p],
            mp=1 - m,
        )

    iota = functools.partial(lax.broadcasted_iota, jnp.int32)
    expand = (2 * (iota((256, 32), 0) // 16) + h == iota((256, 32), 1)).astype(BF)
    in_slot = lax.rem(iota((256, 16), 0), 16) == iota((256, 16), 1)
    mine = (iota((32, 16), 0) == b).astype(BF)
    arrived(0)
    arrived(1)
    counts = countsv[...].astype(F32).astype(BF)
    sent = dot(mine, counts, ((0,), (0,)))
    row = jnp.where(iota((16, 32), 0).astype(F32) < sent, rowsv[...], 384)
    high = (row // 128).astype(F32).astype(BF)
    low = lax.rem(row, 128).astype(F32).astype(BF)
    full = dot(expand, high, ((1,), (1,))) * 128.0 + dot(expand, low, ((1,), (1,)))
    rowc = jnp.sum(jnp.where(in_slot, full, 0.0), axis=1, keepdims=True)
    pick = (rowc == iota((256, 320), 1).astype(F32)).astype(BF)
    arrived(2)
    outg[...] = dot(pick, xv[...]).astype(BF).reshape(16, 16, 256)

    def owner_at(d):
        return lax.rem(2 * lax.rem(z + d, 16) + parity - 4 * r - m + 64, 32) // 2

    def deliver(n, _):
        up = 7 - n
        send(
            outg.at[owner_at(up)],
            fq.at[0, n],
            ss.at[F1],
            rs.at[F1],
            blk=lax.rem(b + 2 * up, 32),
        )
        send(
            outg.at[owner_at(8 + n)],
            fq.at[1, 7 - n],
            ss.at[F1 + 1],
            rs.at[F1 + 1],
            blk=lax.rem(b + 2 * (9 + n), 32),
        )
        return 0

    lax.fori_loop(0, 7, deliver, 0)
    fq[0, 7] = outg[owner_at(0)]
    fq[1, 0] = outg[owner_at(15)]

    def first_z(t, j):
        return lax.rem(t // 2 + (9 if j < 2 else 0), 16)

    held = dot(counts, mine)
    expand_r = (iota((512, 32), 0) // 16 == iota((512, 32), 1)).astype(BF)
    in_slot_r = lax.rem(iota((512, 16), 0), 16) == iota((512, 16), 1)
    alive = dot(expand_r, (iota((32, 16), 1).astype(F32) < held).astype(BF))
    live = jnp.sum(jnp.where(in_slot_r, alive, 0.0), axis=1, keepdims=True) > 0.5
    at = iota((32, 512), 1)
    owner = 4 * (at // 64) + 2 * lax.rem(at // 16, 2) + lax.rem(at // 32, 2)
    expand_t = (owner == iota((32, 512), 0)).astype(BF)
    in_slot_t = lax.rem(iota((16, 512), 1), 16) == iota((16, 512), 0)
    full_t = dot(high, expand_t) * 128.0 + dot(low, expand_t)
    rowr = jnp.sum(jnp.where(in_slot_t, full_t, 0.0), axis=0, keepdims=True)

    arrived(3)
    arrived(4)
    drain(mp_tv, key_rs.at[0])
    drain(mp_mv, key_rs.at[1])
    for i, (src, dst) in enumerate(((mp_tv, mp_ts), (mp_mv, mp_ms))):
        pltpu.make_async_copy(src, dst, key_ls.at[i]).start()
    for i, (src, dst) in enumerate(((mp_tv, mp_ts), (mp_mv, mp_ms))):
        pltpu.make_async_copy(src, dst, key_ls.at[i]).wait()

    def build(p):
        j = m + 2 * p
        pltpu.make_async_copy(
            adj_ref.at[m + 2 * p], vall[p].at[pl.ds(0, 5)], loc_sem.at[p]
        ).wait()
        drain(vall[p].at[pl.ds(5, 5)], adj_rs.at[p])

        def places(ts, ms):
            return [
                jnp.where(ms[j, t] == 1, ts[j, 0, t] * 4 + ts[j, 1, t], 16) for t in range(5)
            ]

        own, other = places(own_ts, own_ms), places(mp_ts, mp_ms)
        for row in range(4):
            for col in range(4):
                at = jnp.int32(10)
                for t in range(5):
                    at = jnp.where(own[t] == row * 4 + col, t, at)
                    at = jnp.where(other[t] == row * 4 + col, 5 + t, at)
                tile = vall[p][at]
                dense[p, row * 128:(row + 1) * 128, col * 128:(col + 1) * 128] = tile

    def transpose(p):
        for row in range(4):
            for col in range(4):
                tile = dense[p, row * 128:(row + 1) * 128, col * 128:(col + 1) * 128]
                denset[p, col * 128:(col + 1) * 128, row * 128:(row + 1) * 128] = tile.T

    def others(p):
        for e in range(1, 4):
            to = lax.rem(m + 2 * p + e, 4)
            yield to, lax.rem(b - m - 2 * p + to + 32, 32)

    build(0)
    for p in range(2):
        drain(fq.at[p, pl.ds(0, 7)], rs.at[F1 + p])
        for to, t in others(p):
            send(
                fq.at[p],
                fr.at[to // 2, m + 2 * p],
                ss.at[XF + p],
                rs.at[XF + to // 2],
                **at_blk(t),
            )
        fr[p, m + 2 * p] = fq[p]
    build(1)

    part = None
    for p in range(2):
        drain(fr.at[p, pl.ds(0, 3)], rs.at[XF + p])
        for j in range(4):
            t = lax.rem(b - m - 2 * p + j + 32, 32)
            for n in range(8):
                nat[p, lax.rem(first_z(t, j) + n, 16), lax.rem(t, 2)] = fr[p, j, n]
        term = dot(dense[p], nat[p].reshape(512, 256))
        part = term if part is None else part + term

    r1s[...] = part.astype(BF).reshape(16, 32, 256)

    def scatter(d, _):
        tr, tm = in_group(d)
        send(r1s.at[2 * tr + tm], r1r.at[k], ss.at[R1], rs.at[R1], rep=tr, mp=tm)
        return 0

    lax.fori_loop(1, 16, scatter, 0)
    r1r[k] = r1s[k]
    transpose(0)
    drain(r1r.at[pl.ds(0, 15)], rs.at[R1])
    total = r1r[0].astype(F32)
    for i in range(1, 16):
        total += r1r[i].astype(F32)
    agg[k] = total.astype(BF)

    def gather(d, _):
        tr, tm = in_group(d)
        send(agg.at[k], agg.at[k], ss.at[R2], rs.at[R2], rep=tr, mp=tm)
        return 0

    lax.fori_loop(1, 16, gather, 0)
    transpose(1)
    arrived(5)
    arrived(6)
    drain(agg.at[pl.ds(0, 15)], rs.at[R2])

    for q in range(4):
        rows = slice(q * 128, (q + 1) * 128)
        preact = dot(agg[4 * q:4 * q + 4].reshape(128, 256), wv[...])
        gate = jax.nn.sigmoid(preact)
        hidv[rows, :] = jnp.where(live[rows], preact * gate, 0.0).astype(BF)
        slope = gate * (1.0 + preact * (1.0 - gate))
        pre = jnp.where(live[rows], ogv[rows, :].astype(F32) * slope, 0.0).astype(BF)
        pg[rows, :] = pre
        gb[rows, :] = dot(pre, wv[...], ((1,), (1,))).astype(BF)

    for p in range(2):
        terms = dot(denset[p], gb[...]).astype(BF).reshape(16, 2, 16, 256)
        for q in range(2):
            pb[p, q, 0:16] = terms[:, q]
            pb[p, q, 16:24] = terms[0:8, q]
        for to, t in others(p):
            start = lax.rem(t // 2 + jnp.where(to < 2, 9, 0), 16)
            send(
                pb.at[p, lax.rem(t, 2), pl.ds(start, 8)],
                xr.at[to // 2, m + 2 * p],
                ss.at[XB + p],
                rs.at[XB + to // 2],
                **at_blk(t),
            )
        xr[p, m + 2 * p] = pb[p, parity, pl.ds(first_z(b, 2 * p), 8)]
    pltpu.make_async_copy(hidv, hid_ref, out_sem.at[0]).start()

    columns = pl.ds(pl.multiple_of((r // 4) * 128, 128), 128)
    wprod[...] = dot(agg[:, :, columns].reshape(512, 128), pg[...], ((0,), (0,))).reshape(8, 16, 256)
    w16 = wprod[lax.rem(r, 4) * 2 + h]
    for a in range(2):
        for c in range(2):
            wa[2 * a + c] = w16[a * 8:(a + 1) * 8, c * 128:(c + 1) * 128]
    war[quad] = wa[quad]
    for e in range(1, 4):
        q = lax.rem(quad + e, 4)
        send(wa.at[q], war.at[quad], ss.at[WA], rs.at[WA], **at_blk(b - quad + q))
    eighth = b // 4

    for p in range(2):
        drain(xr.at[p, pl.ds(0, 3)], rs.at[XB + p])
        total = xr[p, 0].astype(F32)
        for i in range(1, 4):
            total += xr[p, i].astype(F32)
        mb[p] = total.astype(BF)
        if p == 0:
            drain(war.at[pl.ds(0, 3)], rs.at[WA])
            tile = war[0] + war[1] + war[2] + war[3]
            wb[...] = tile
            wbr[eighth] = tile
            for e in range(1, 8):
                send(wb, wbr.at[eighth], ss.at[WB], rs.at[WB], blk=lax.rem(b + 4 * e, 32))
        c = lax.rem(b - 4 * r - m - 2 * p + 64, 32)
        home, slot = c // 4, lax.rem(c, 4) // 2

        def back(n, _):
            away = 7 - n
            send(
                mb.at[p, n if p == 0 else away],
                ar.at[slot, r],
                ss.at[A2S + p],
                rs.at[A2],
                blk=lax.rem(b + (32 - 2 * away if p == 0 else 2 * away), 32),
                rep=home,
            )
            return 0

        lax.fori_loop(0, 7, back, 0)
        here = 7 if p == 0 else 0

        @pl.when(home == r)
        def _():
            pltpu.make_async_copy(mb.at[p, here], ar.at[slot, r], rs.at[A2]).start()

        @pl.when(home != r)
        def _():
            send(mb.at[p, here], ar.at[slot, r], ss.at[SELF + p], rs.at[A2], rep=home)

    place = (rowr == iota((320, 512), 0).astype(F32)).astype(BF)
    drain(wbr.at[pl.ds(0, 7)], rs.at[WB])
    tile = wbr[0]
    for i in range(1, 8):
        tile += wbr[i]
    wc[quad] = tile
    for e in range(1, 4):
        q = lax.rem(quad + e, 4)
        send(wc.at[quad], wc.at[quad], ss.at[WC], rs.at[WC], **at_blk(b - quad + q))

    drain(ar, rs.at[A2])
    total = ar[:, 0].astype(F32)
    for i in range(1, 8):
        total += ar[:, i].astype(F32)
    gg[kw] = total.astype(BF)

    def share(d, _):
        tr, tm = in_group(d)
        send(gg.at[kw], gg.at[kw], ss.at[G], rs.at[G], rep=tr, mp=tm)
        return 0

    lax.fori_loop(1, 16, share, 0)

    drain(wc.at[pl.ds(0, 3)], rs.at[WC])
    for a in range(2):
        for c in range(2):
            w_part = wc[2 * a + c]
            wprod[0, a * 8:(a + 1) * 8, c * 128:(c + 1) * 128] = w_part
    wd[kw] = wprod[0].astype(BF)

    def spread_w(d, _):
        tr, tm = in_group(d)
        send(wd.at[kw], wd.at[kw], ss.at[WD], rs.at[WD], rep=tr, mp=tm)
        return 0

    lax.fori_loop(1, 16, spread_w, 0)

    drain(gg.at[pl.ds(0, 15)], rs.at[G])
    igv[...] = dot(place, gg[...].reshape(512, 256))
    pltpu.make_async_copy(igv, ig_ref, out_sem.at[1]).start()
    drain(wd.at[pl.ds(0, 15)], rs.at[WD])
    wgv[...] = wd[...].reshape(256, 256).astype(F32) * (1.0 / 128.0)
    pltpu.make_async_copy(wgv, wg_ref, out_sem.at[2]).start()

    drain(mp_tv, key_ss.at[0])
    drain(mp_mv, key_ss.at[1])
    for p in range(2):
        drain(vall[p].at[pl.ds(5, 5)], adj_ss.at[p])
        drain(fq.at[p, pl.ds(0, 7)], ss.at[F1 + p])
        drain(fr.at[p, pl.ds(0, 3)], ss.at[XF + p])
        drain(xr.at[p, pl.ds(0, 3)], ss.at[XB + p])
        drain(mb.at[p, pl.ds(0, 7)], ss.at[A2S + p])
        c = lax.rem(b - 4 * r - m - 2 * p + 64, 32)

        @pl.when(c // 4 != r)
        def _():
            drain(mb.at[p, 0], ss.at[SELF + p])

    drain(r1r.at[pl.ds(0, 15)], ss.at[R1])
    drain(agg.at[pl.ds(0, 15)], ss.at[R2])
    drain(gg.at[pl.ds(0, 15)], ss.at[G])
    drain(wa.at[pl.ds(0, 3)], ss.at[WA])
    drain(wbr.at[pl.ds(0, 7)], ss.at[WB])
    drain(wc.at[pl.ds(0, 3)], ss.at[WC])
    drain(wd.at[pl.ds(0, 15)], ss.at[WD])
    for i, (src, dst) in enumerate(((hidv, hid_ref), (igv, ig_ref), (wgv, wg_ref))):
        pltpu.make_async_copy(src, dst, out_sem.at[i]).wait()


def hand_over(a0, a1, a2, o0, o1, o2, v0, v1, v2, sem):
    trips = ((a0, v0, o0), (a1, v1, o1), (a2, v2, o2))
    for i, (src, mid, _) in enumerate(trips):
        pltpu.make_async_copy(src, mid, sem.at[i]).start()
    for i, (src, mid, dst) in enumerate(trips):
        pltpu.make_async_copy(src, mid, sem.at[i]).wait()
        pltpu.make_async_copy(mid, dst, sem.at[3 + i]).start()
    for i, (_, mid, dst) in enumerate(trips):
        pltpu.make_async_copy(mid, dst, sem.at[3 + i]).wait()


def shards(x_in, weight, out_grad, adj_vals, adj_tiles, adj_mask, send_rows, send_counts):
    hbm = pl.BlockSpec(memory_space=pltpu.HBM)
    V = pltpu.VMEM
    S = pltpu.SMEM
    I32 = jnp.int32
    dma = pltpu.SemaphoreType.DMA
    outs = (
        jax.ShapeDtypeStruct((512, 256), BF),
        jax.ShapeDtypeStruct((256, 256), F32),
        jax.ShapeDtypeStruct((320, 256), F32),
    )
    results = pl.pallas_call(
        kernel,
        out_shape=outs,
        in_specs=[hbm] * 8,
        out_specs=(hbm,) * 3,
        scratch_shapes=[V((11, 128, 128), BF)] * 2
        + [
            V((320, 256), BF),
            V((256, 256), BF),
            V((512, 256), BF),
            V((16, 32), I32),
            V((32, 32), I32),
            S((4, 2, 5), I32),
            S((4, 5), I32),
            V((4, 2, 5), I32),
            V((4, 5), I32),
            S((4, 2, 5), I32),
            S((4, 5), I32),
            V((2, 512, 512), BF),
            V((2, 512, 512), BF),
            V((16, 16, 256), BF),
            V((2, 8, 16, 256), BF),
            V((2, 4, 8, 16, 256), BF),
            V((2, 16, 2, 16, 256), BF),
            V((16, 32, 256), BF),
            V((16, 32, 256), BF),
            V((16, 32, 256), BF),
            V((512, 256), BF),
            V((512, 256), BF),
            V((2, 2, 24, 16, 256), BF),
            V((2, 4, 8, 16, 256), BF),
            V((2, 8, 16, 256), BF),
            V((2, 8, 16, 256), BF),
            V((16, 2, 16, 256), BF),
            V((8, 16, 256), F32),
            V((4, 8, 128), F32),
            V((4, 8, 128), F32),
            V((8, 128), F32),
            V((8, 8, 128), F32),
            V((4, 8, 128), F32),
            V((16, 16, 256), BF),
            V((512, 256), BF),
            V((256, 256), F32),
            V((320, 256), F32),
            dma((2,)),
            dma((7,)),
            dma((3,)),
            dma((2,)),
            dma((2,)),
            dma((2,)),
            dma((2,)),
            dma((2,)),
            dma((18,)),
            dma((18,)),
        ],
        compiler_params=pltpu.CompilerParams(
            collective_id=0, has_side_effects=True, vmem_limit_bytes=62 * 1024 * 1024
        ),
        name="graph_layer",
    )(
        jnp.swapaxes(adj_tiles[0], 1, 2),
        adj_mask[0],
        x_in,
        weight,
        out_grad,
        send_rows[0].T,
        send_counts,
        adj_vals[0],
    )
    return pl.pallas_call(
        hand_over,
        out_shape=outs,
        in_specs=[pl.BlockSpec(memory_space=pl.ANY)] * 3,
        out_specs=(hbm,) * 3,
        scratch_shapes=[V(o.shape, o.dtype) for o in outs] + [dma((6,))],
        compiler_params=pltpu.CompilerParams(vmem_limit_bytes=62 * 1024 * 1024),
        name="hand_over",
    )(*results)


def solution(mesh):
    placed = (
        P("blk", None),
        P(),
        P("blk", None),
        P("blk", "rep", "mp", None, None),
        P("blk", "rep", "mp", None),
        P("blk", "rep", "mp"),
        P("blk", None, None),
        P(),
    )
    return jax.shard_map(
        shards,
        mesh=mesh,
        in_specs=placed,
        out_specs=(P("blk", None), P(), P("blk", None)),
        check_vma=False,
    )
```

time: 82.4 us -> 75.1 us (0.911)
  Pallas kernels: 81.6 us -> 74.4 us
    pallas_call x1, Pallas kernels: 79.7 us -> 72.5 us  [shards(): pl.pallas_call(kernel, out_shape=outs, in_specs=[hbm] * 8, out_specs=(hbm...]
where the time goes in v3:
time: 75.1 us; the launch traced here: 75 us
  Pallas kernels  74.4 us (99%)
    pallas_call x1, Pallas kernels, shards(): pl.pallas_call(kernel, out_shape=outs, in_specs=[hbm] * 8, out_specs=(hbm...  72.5 us
    pallas_call x1, Pallas kernels, shards(): pl.pallas_call(hand_over, out_shape=outs, in_specs=[pl.BlockSpec(memory_s...  1.91 us

profile of v3, /device:TPU:1, one launch (start us, length us, event | category | flops | bytes accessed | tf_op | source)
XLA Modules:
  0.0 75.0 jit_solution(7052234911550650043)
XLA Ops:
  0.6 72.5 %graph_layer.1 = (bf16[512,256]{1,0:T(8,128)(2,1)}, f32[256,256]{1,0:T(8,128)}, f32[320,256]{1,0:T(8,128)}) custom-call(s32[4,2,5]{2,1,0:T(2,128)} %bitcast.10, s32[4,5]{1,0:T(4,128)} %bitcast.11, bf16[320,256]{1,0:T(8,128)(2,1)} %x_ref.1, bf16[256,256]{1,0:T(8,128)(2,1)} %w_ref.1, bf16[512,256]{1,0:T(8,128)(2,1)} %og_ref.1, s32[16,32]{1,0:T(8,128)} %bitcast.9, ...), custom_call_target="tpu_custom_call" | custom-call | tf_op jit(solution)/shard_map/graph_layer/pallas_call | solution.py:456
  73.1 1.9 %hand_over.1 = (bf16[512,256]{1,0:T(8,128)(2,1)}, f32[256,256]{1,0:T(8,128)}, f32[320,256]{1,0:T(8,128)}) custom-call(bf16[512,256]{1,0:T(8,128)(2,1)} %get-tuple-element.6.a0, f32[256,256]{1,0:T(8,128)} %get-tuple-element.7.a1, f32[320,256]{1,0:T(8,128)} %get-tuple-element.8.a2), custom_call_target="tpu_custom_call" | custom-call | tf_op jit(solution)/shard_map/hand_over/pallas_call | solution.py:525

commit v4 on v3

--- a/solution.py
+++ b/solution.py
@@ -41,8 +41,9 @@
     counts_ref,
     adj_ref,
     hid_ref,
-    wg_ref,
-    ig_ref,
+    rowr_ref,
+    gg_ref,
+    wd_ref,
     v0, v1,
     xv, wv, ogv, rowsv, countsv,
     own_ts, own_ms, mp_tv, mp_mv, mp_ts, mp_ms,
@@ -50,9 +51,9 @@
     outg, fq, fr, nat,
     r1s, r1r, agg,
     pg, gb,
-    pb, xr, mb, ar, gg,
-    wprod, wa, war, wb, wbr, wc, wd,
-    hidv, wgv, igv,
+    pb, xr, mb, ar, gv,
+    wprod, wa, war, wb, wbr, wc, wdv,
+    hidv, rowrv,
     loc_sem, in_sem, out_sem, adj_ss, adj_rs, key_ss, key_rs, key_ls,
     ss, rs,
 ):
@@ -67,7 +68,7 @@
     kw = r * 2 + h
     quad = lax.rem(b, 4)
     R1, R2, G, WA, WB, WC, WD, A2 = range(8)
-    F1, XF, XB, A2S, SELF = 8, 10, 12, 14, 16
+    XF, XB, A2S, SELF, F1 = 8, 10, 12, 14, 16
 
     def at_blk(t):
         return {"blk": t, "mp": lax.rem(h + t, 2)}
@@ -75,29 +76,6 @@
     def in_group(d):
         t = lax.rem(k + d, 16)
         return t // 2, lax.rem(t, 2)
-
-    barrier = pltpu.get_barrier_semaphore()
-
-    def greet(where):
-        pl.semaphore_signal(barrier, inc=1, device_id=where, device_id_type=MESH)
-
-    greet({"blk": lax.rem(b + 16, 32)})
-
-    def greet_z(n, _):
-        greet({"blk": lax.rem(b + 14 - 2 * n, 32)})
-        greet({"blk": lax.rem(b + 18 + 2 * n, 32)})
-        return 0
-
-    lax.fori_loop(0, 7, greet_z, 0)
-
-    def greet_group(d, _):
-        tr, tm = in_group(d)
-        greet({"rep": tr, "mp": tm})
-        return 0
-
-    lax.fori_loop(1, 16, greet_group, 0)
-    for d in (29, 3, 31, 1):
-        greet(at_blk(lax.rem(b + d, 32)))
 
     staged = (
         (rows_ref, rowsv),
@@ -108,8 +86,37 @@
         (w_ref, wv),
         (og_ref, ogv),
     )
-    for i, (src, dst) in enumerate(staged):
-        pltpu.make_async_copy(src, dst, in_sem.at[i]).start()
+
+    def start(first, end):
+        for i in range(first, end):
+            src, dst = staged[i]
+            pltpu.make_async_copy(src, dst, in_sem.at[i]).start()
+
+    start(0, 3)
+
+    barrier = pltpu.get_barrier_semaphore()
+
+    def greet(where):
+        pl.semaphore_signal(barrier, inc=1, device_id=where, device_id_type=MESH)
+
+    def greet_z(n, _):
+        greet({"blk": lax.rem(b + 14 - 2 * n, 32)})
+        greet({"blk": lax.rem(b + 18 + 2 * n, 32)})
+        return 0
+
+    lax.fori_loop(0, 7, greet_z, 0)
+
+    for d in (29, 3, 31, 1):
+        greet(at_blk(lax.rem(b + d, 32)))
+    greet({"mp": 1 - m})
+
+    def greet_rep(d, _):
+        greet({"rep": lax.rem(r + d, 8)})
+        return 0
+
+    lax.fori_loop(1, 8, greet_rep, 0)
+
+    start(3, 7)
 
     def arrived(i):
         src, dst = staged[i]
@@ -120,19 +127,6 @@
             adj_ref.at[m + 2 * p], vall[p].at[pl.ds(0, 5)], loc_sem.at[p]
         ).start()
         vall[p][10] = jnp.zeros((128, 128), BF)
-
-    pl.semaphore_wait(barrier, 34)
-
-    send(tiles_ref, mp_tv, key_ss.at[0], key_rs.at[0], mp=1 - m)
-    send(mask_ref, mp_mv, key_ss.at[1], key_rs.at[1], mp=1 - m)
-    for p in range(2):
-        send(
-            adj_ref.at[1 - m + 2 * p],
-            vall[p].at[pl.ds(5, 5)],
-            adj_ss.at[p],
-            adj_rs.at[p],
-            mp=1 - m,
-        )
 
     iota = functools.partial(lax.broadcasted_iota, jnp.int32)
     expand = (2 * (iota((256, 32), 0) // 16) + h == iota((256, 32), 1)).astype(BF)
@@ -151,28 +145,46 @@
     arrived(2)
     outg[...] = dot(pick, xv[...]).astype(BF).reshape(16, 16, 256)
 
+    pl.semaphore_wait(barrier, 26)
+
     def owner_at(d):
         return lax.rem(2 * lax.rem(z + d, 16) + parity - 4 * r - m + 64, 32) // 2
 
-    def deliver(n, _):
-        up = 7 - n
+    def deliver(far):
+        def one(n, _):
+            up = 7 - n
+            low, top = F1 + 1 - far, F1 + 2 + far
+            send(
+                outg.at[owner_at(up)],
+                fq.at[0, n],
+                ss.at[low],
+                rs.at[low],
+                blk=lax.rem(b + 2 * up, 32),
+            )
+            send(
+                outg.at[owner_at(8 + n)],
+                fq.at[1, 7 - n],
+                ss.at[top],
+                rs.at[top],
+                blk=lax.rem(b + 2 * (9 + n), 32),
+            )
+            return 0
+
+        lax.fori_loop(*((0, 4) if far else (4, 7)), one, 0)
+
+    deliver(1)
+    deliver(0)
+
+    send(tiles_ref, mp_tv, key_ss.at[0], key_rs.at[0], mp=1 - m)
+    send(mask_ref, mp_mv, key_ss.at[1], key_rs.at[1], mp=1 - m)
+    for p in range(2):
         send(
-            outg.at[owner_at(up)],
-            fq.at[0, n],
-            ss.at[F1],
-            rs.at[F1],
-            blk=lax.rem(b + 2 * up, 32),
+            adj_ref.at[1 - m + 2 * p],
+            vall[p].at[pl.ds(5, 5)],
+            adj_ss.at[p],
+            adj_rs.at[p],
+            mp=1 - m,
         )
-        send(
-            outg.at[owner_at(8 + n)],
-            fq.at[1, 7 - n],
-            ss.at[F1 + 1],
-            rs.at[F1 + 1],
-            blk=lax.rem(b + 2 * (9 + n), 32),
-        )
-        return 0
-
-    lax.fori_loop(0, 7, deliver, 0)
     fq[0, 7] = outg[owner_at(0)]
     fq[1, 0] = outg[owner_at(15)]
 
@@ -189,7 +201,8 @@
     expand_t = (owner == iota((32, 512), 0)).astype(BF)
     in_slot_t = lax.rem(iota((16, 512), 1), 16) == iota((16, 512), 0)
     full_t = dot(high, expand_t) * 128.0 + dot(low, expand_t)
-    rowr = jnp.sum(jnp.where(in_slot_t, full_t, 0.0), axis=0, keepdims=True)
+    rowrv[...] = jnp.sum(jnp.where(in_slot_t, full_t, 0.0), axis=0, keepdims=True)
+    pltpu.make_async_copy(rowrv, rowr_ref, out_sem.at[1]).start()
 
     arrived(3)
     arrived(4)
@@ -229,24 +242,28 @@
                 denset[p, col * 128:(col + 1) * 128, row * 128:(row + 1) * 128] = tile.T
 
     def others(p):
-        for e in range(1, 4):
-            to = lax.rem(m + 2 * p + e, 4)
-            yield to, lax.rem(b - m - 2 * p + to + 32, 32)
+        for q, to in ((p, 1 - m + 2 * p), (1 - p, 2 * p), (1 - p, 2 * p + 1)):
+            yield q, to, lax.rem(b - m - 2 * q + to + 32, 32)
+
+    for far in (1, 0):
+        for p in range(2):
+            sem = F1 + 2 * p + (far if p else 1 - far)
+            drain(fq.at[p, pl.ds(0, 3 + far)], rs.at[sem])
+        for p in range(2):
+            for q, to, t in others(p):
+                piece = pl.ds(4 * (far if q else 1 - far), 4)
+                send(
+                    fq.at[q, piece],
+                    fr.at[p, m + 2 * q, piece],
+                    ss.at[XF + q],
+                    rs.at[XF + p],
+                    **at_blk(t),
+                )
+    for p in range(2):
+        fr[p, m + 2 * p] = fq[p]
 
     build(0)
-    for p in range(2):
-        drain(fq.at[p, pl.ds(0, 7)], rs.at[F1 + p])
-        for to, t in others(p):
-            send(
-                fq.at[p],
-                fr.at[to // 2, m + 2 * p],
-                ss.at[XF + p],
-                rs.at[XF + to // 2],
-                **at_blk(t),
-            )
-        fr[p, m + 2 * p] = fq[p]
     build(1)
-
     part = None
     for p in range(2):
         drain(fr.at[p, pl.ds(0, 3)], rs.at[XF + p])
@@ -293,23 +310,6 @@
         pre = jnp.where(live[rows], ogv[rows, :].astype(F32) * slope, 0.0).astype(BF)
         pg[rows, :] = pre
         gb[rows, :] = dot(pre, wv[...], ((1,), (1,))).astype(BF)
-
-    for p in range(2):
-        terms = dot(denset[p], gb[...]).astype(BF).reshape(16, 2, 16, 256)
-        for q in range(2):
-            pb[p, q, 0:16] = terms[:, q]
-            pb[p, q, 16:24] = terms[0:8, q]
-        for to, t in others(p):
-            start = lax.rem(t // 2 + jnp.where(to < 2, 9, 0), 16)
-            send(
-                pb.at[p, lax.rem(t, 2), pl.ds(start, 8)],
-                xr.at[to // 2, m + 2 * p],
-                ss.at[XB + p],
-                rs.at[XB + to // 2],
-                **at_blk(t),
-            )
-        xr[p, m + 2 * p] = pb[p, parity, pl.ds(first_z(b, 2 * p), 8)]
-    pltpu.make_async_copy(hidv, hid_ref, out_sem.at[0]).start()
 
     columns = pl.ds(pl.multiple_of((r // 4) * 128, 128), 128)
     wprod[...] = dot(agg[:, :, columns].reshape(512, 128), pg[...], ((0,), (0,))).reshape(8, 16, 256)
@@ -324,18 +324,35 @@
     eighth = b // 4
 
     for p in range(2):
+        terms = dot(denset[p], gb[...]).astype(BF).reshape(16, 2, 16, 256)
+        for q in range(2):
+            pb[p, q, 0:16] = terms[:, q]
+            pb[p, q, 16:24] = terms[0:8, q]
+        xr[p, m + 2 * p] = pb[p, parity, pl.ds(first_z(b, 2 * p), 8)]
+    for p in range(2):
+        for q, to, t in others(p):
+            send(
+                pb.at[q, lax.rem(t, 2), pl.ds(first_z(t, 2 * p), 8)],
+                xr.at[p, m + 2 * q],
+                ss.at[XB + q],
+                rs.at[XB + p],
+                **at_blk(t),
+            )
+    pltpu.make_async_copy(hidv, hid_ref, out_sem.at[0]).start()
+
+    drain(war.at[pl.ds(0, 3)], rs.at[WA])
+    tile = war[0] + war[1] + war[2] + war[3]
+    wb[...] = tile
+    wbr[eighth] = tile
+    for e in range(1, 8):
+        send(wb, wbr.at[eighth], ss.at[WB], rs.at[WB], blk=lax.rem(b + 4 * e, 32))
+
+    for p in range(2):
         drain(xr.at[p, pl.ds(0, 3)], rs.at[XB + p])
         total = xr[p, 0].astype(F32)
         for i in range(1, 4):
             total += xr[p, i].astype(F32)
         mb[p] = total.astype(BF)
-        if p == 0:
-            drain(war.at[pl.ds(0, 3)], rs.at[WA])
-            tile = war[0] + war[1] + war[2] + war[3]
-            wb[...] = tile
-            wbr[eighth] = tile
-            for e in range(1, 8):
-                send(wb, wbr.at[eighth], ss.at[WB], rs.at[WB], blk=lax.rem(b + 4 * e, 32))
         c = lax.rem(b - 4 * r - m - 2 * p + 64, 32)
         home, slot = c // 4, lax.rem(c, 4) // 2
 
@@ -362,7 +379,6 @@
         def _():
             send(mb.at[p, here], ar.at[slot, r], ss.at[SELF + p], rs.at[A2], rep=home)
 
-    place = (rowr == iota((320, 512), 0).astype(F32)).astype(BF)
     drain(wbr.at[pl.ds(0, 7)], rs.at[WB])
     tile = wbr[0]
     for i in range(1, 8):
@@ -372,45 +388,44 @@
         q = lax.rem(quad + e, 4)
         send(wc.at[quad], wc.at[quad], ss.at[WC], rs.at[WC], **at_blk(b - quad + q))
 
-    drain(ar, rs.at[A2])
-    total = ar[:, 0].astype(F32)
-    for i in range(1, 8):
-        total += ar[:, i].astype(F32)
-    gg[kw] = total.astype(BF)
-
-    def share(d, _):
-        tr, tm = in_group(d)
-        send(gg.at[kw], gg.at[kw], ss.at[G], rs.at[G], rep=tr, mp=tm)
-        return 0
-
-    lax.fori_loop(1, 16, share, 0)
-
     drain(wc.at[pl.ds(0, 3)], rs.at[WC])
     for a in range(2):
         for c in range(2):
             w_part = wc[2 * a + c]
             wprod[0, a * 8:(a + 1) * 8, c * 128:(c + 1) * 128] = w_part
-    wd[kw] = wprod[0].astype(BF)
+    wdv[...] = wprod[0].astype(BF)
+    pltpu.make_async_copy(wdv, wd_ref.at[kw], rs.at[WD]).start()
 
     def spread_w(d, _):
         tr, tm = in_group(d)
-        send(wd.at[kw], wd.at[kw], ss.at[WD], rs.at[WD], rep=tr, mp=tm)
+        send(wdv, wd_ref.at[kw], ss.at[WD], rs.at[WD], rep=tr, mp=tm)
         return 0
 
     lax.fori_loop(1, 16, spread_w, 0)
 
-    drain(gg.at[pl.ds(0, 15)], rs.at[G])
-    igv[...] = dot(place, gg[...].reshape(512, 256))
-    pltpu.make_async_copy(igv, ig_ref, out_sem.at[1]).start()
-    drain(wd.at[pl.ds(0, 15)], rs.at[WD])
-    wgv[...] = wd[...].reshape(256, 256).astype(F32) * (1.0 / 128.0)
-    pltpu.make_async_copy(wgv, wg_ref, out_sem.at[2]).start()
+    drain(ar, rs.at[A2])
+    total = ar[:, 0].astype(F32)
+    for i in range(1, 8):
+        total += ar[:, i].astype(F32)
+    gv[...] = total.astype(BF)
+    pltpu.make_async_copy(gv, gg_ref.at[kw], rs.at[G]).start()
+
+    def share(d, _):
+        tr, tm = in_group(d)
+        send(gv, gg_ref.at[kw], ss.at[G], rs.at[G], rep=tr, mp=tm)
+        return 0
+
+    lax.fori_loop(1, 16, share, 0)
+
+    drain(wd_ref, rs.at[WD])
+    drain(gg_ref, rs.at[G])
 
     drain(mp_tv, key_ss.at[0])
     drain(mp_mv, key_ss.at[1])
     for p in range(2):
         drain(vall[p].at[pl.ds(5, 5)], adj_ss.at[p])
-        drain(fq.at[p, pl.ds(0, 7)], ss.at[F1 + p])
+        drain(fq.at[p, pl.ds(0, 4 if p == 0 else 3)], ss.at[F1 + 2 * p])
+        drain(fq.at[p, pl.ds(0, 3 if p == 0 else 4)], ss.at[F1 + 2 * p + 1])
         drain(fr.at[p, pl.ds(0, 3)], ss.at[XF + p])
         drain(xr.at[p, pl.ds(0, 3)], ss.at[XB + p])
         drain(mb.at[p, pl.ds(0, 7)], ss.at[A2S + p])
@@ -422,24 +437,37 @@
 
     drain(r1r.at[pl.ds(0, 15)], ss.at[R1])
     drain(agg.at[pl.ds(0, 15)], ss.at[R2])
-    drain(gg.at[pl.ds(0, 15)], ss.at[G])
+    drain(gg_ref.at[pl.ds(0, 15)], ss.at[G])
     drain(wa.at[pl.ds(0, 3)], ss.at[WA])
     drain(wbr.at[pl.ds(0, 7)], ss.at[WB])
     drain(wc.at[pl.ds(0, 3)], ss.at[WC])
-    drain(wd.at[pl.ds(0, 15)], ss.at[WD])
-    for i, (src, dst) in enumerate(((hidv, hid_ref), (igv, ig_ref), (wgv, wg_ref))):
+    drain(wd_ref.at[pl.ds(0, 15)], ss.at[WD])
+    for i, (src, dst) in enumerate(((hidv, hid_ref), (rowrv, rowr_ref))):
         pltpu.make_async_copy(src, dst, out_sem.at[i]).wait()
 
 
-def hand_over(a0, a1, a2, o0, o1, o2, v0, v1, v2, sem):
-    trips = ((a0, v0, o0), (a1, v1, o1), (a2, v2, o2))
-    for i, (src, mid, _) in enumerate(trips):
-        pltpu.make_async_copy(src, mid, sem.at[i]).start()
-    for i, (src, mid, dst) in enumerate(trips):
-        pltpu.make_async_copy(src, mid, sem.at[i]).wait()
-        pltpu.make_async_copy(mid, dst, sem.at[3 + i]).start()
-    for i, (_, mid, dst) in enumerate(trips):
-        pltpu.make_async_copy(mid, dst, sem.at[3 + i]).wait()
+def finish(hid_in, rowr_in, gg_in, wd_in, hid_ref, wg_ref, ig_ref, hid, rowr, gg, wd, wg, ig, sem):
+    incoming = ((rowr_in, rowr), (gg_in, gg), (wd_in, wd), (hid_in, hid))
+    outgoing = ((ig, ig_ref), (wg, wg_ref), (hid, hid_ref))
+    for i, (src, dst) in enumerate(incoming):
+        pltpu.make_async_copy(src, dst, sem.at[i]).start()
+
+    def arrived(i):
+        src, dst = incoming[i]
+        pltpu.make_async_copy(src, dst, sem.at[i]).wait()
+
+    arrived(0)
+    place = (rowr[...] == lax.broadcasted_iota(jnp.int32, (320, 512), 0).astype(F32)).astype(BF)
+    arrived(1)
+    ig[...] = dot(place, gg[...].reshape(512, 256))
+    pltpu.make_async_copy(*outgoing[0], sem.at[4]).start()
+    arrived(2)
+    wg[...] = wd[...].reshape(256, 256).astype(F32) * (1.0 / 128.0)
+    pltpu.make_async_copy(*outgoing[1], sem.at[5]).start()
+    arrived(3)
+    pltpu.make_async_copy(*outgoing[2], sem.at[6]).start()
+    for i, (src, dst) in enumerate(outgoing):
+        pltpu.make_async_copy(src, dst, sem.at[4 + i]).wait()
 
 
 def shards(x_in, weight, out_grad, adj_vals, adj_tiles, adj_mask, send_rows, send_counts):
@@ -453,11 +481,17 @@
         jax.ShapeDtypeStruct((256, 256), F32),
         jax.ShapeDtypeStruct((320, 256), F32),
     )
+    between = (
+        jax.ShapeDtypeStruct((512, 256), BF),
+        jax.ShapeDtypeStruct((1, 512), F32),
+        jax.ShapeDtypeStruct((16, 2, 16, 256), BF),
+        jax.ShapeDtypeStruct((16, 16, 256), BF),
+    )
     results = pl.pallas_call(
         kernel,
-        out_shape=outs,
+        out_shape=between,
         in_specs=[hbm] * 8,
-        out_specs=(hbm,) * 3,
+        out_specs=(hbm,) * 4,
         scratch_shapes=[V((11, 128, 128), BF)] * 2
         + [
             V((320, 256), BF),
@@ -486,27 +520,26 @@
             V((2, 4, 8, 16, 256), BF),
             V((2, 8, 16, 256), BF),
             V((2, 8, 16, 256), BF),
-            V((16, 2, 16, 256), BF),
+            V((2, 16, 256), BF),
             V((8, 16, 256), F32),
             V((4, 8, 128), F32),
             V((4, 8, 128), F32),
             V((8, 128), F32),
             V((8, 8, 128), F32),
             V((4, 8, 128), F32),
-            V((16, 16, 256), BF),
+            V((16, 256), BF),
             V((512, 256), BF),
-            V((256, 256), F32),
-            V((320, 256), F32),
+            V((1, 512), F32),
             dma((2,)),
             dma((7,)),
-            dma((3,)),
-            dma((2,)),
-            dma((2,)),
-            dma((2,)),
-            dma((2,)),
-            dma((2,)),
-            dma((18,)),
-            dma((18,)),
+            dma((2,)),
+            dma((2,)),
+            dma((2,)),
+            dma((2,)),
+            dma((2,)),
+            dma((2,)),
+            dma((20,)),
+            dma((20,)),
         ],
         compiler_params=pltpu.CompilerParams(
             collective_id=0, has_side_effects=True, vmem_limit_bytes=62 * 1024 * 1024
@@ -523,13 +556,13 @@
         adj_vals[0],
     )
     return pl.pallas_call(
-        hand_over,
+        finish,
         out_shape=outs,
-        in_specs=[pl.BlockSpec(memory_space=pl.ANY)] * 3,
+        in_specs=[hbm] * 4,
         out_specs=(hbm,) * 3,
-        scratch_shapes=[V(o.shape, o.dtype) for o in outs] + [dma((6,))],
+        scratch_shapes=[V(o.shape, o.dtype) for o in between + outs[1:]] + [dma((7,))],
         compiler_params=pltpu.CompilerParams(vmem_limit_bytes=62 * 1024 * 1024),
-        name="hand_over",
+        name="finish",
     )(*results)
 
 

time: 75.1 us -> 72.7 us (0.968)
  Pallas kernels: 74.4 us -> 71.9 us
    pallas_call x2, Pallas kernels: 74.4 us -> 71.9 us  [the longest x1 69.7 us: shards(): pl.pallas_call(kernel, out_shape=between, in_specs=[hbm] * 8, out_specs=(...]
where the time goes in v4:
time: 72.7 us; the launch traced here: 72.5 us
  Pallas kernels  71.9 us (99%)
    pallas_call x1, Pallas kernels, shards(): pl.pallas_call(kernel, out_shape=between, in_specs=[hbm] * 8, out_specs=(...  69.7 us
    pallas_call x1, Pallas kernels, shards(): pl.pallas_call(finish, out_shape=outs, in_specs=[hbm] * 4, out_specs=(hbm...  2.16 us

profile of v4, /device:TPU:1, one launch (start us, length us, event | category | flops | bytes accessed | tf_op | source)
XLA Modules:
  0.0 72.5 jit_solution(707333236767952642)
XLA Ops:
  0.6 69.7 %graph_layer.1 = (bf16[512,256]{1,0:T(8,128)(2,1)}, f32[1,512]{1,0:T(1,128)}, bf16[16,2,16,256]{3,2,1,0:T(8,128)(2,1)}, bf16[16,16,256]{2,1,0:T(8,128)(2,1)}) custom-call(s32[4,2,5]{2,1,0:T(2,128)} %bitcast.10, s32[4,5]{1,0:T(4,128)} %bitcast.11, bf16[320,256]{1,0:T(8,128)(2,1)} %x_ref.1, bf16[256,256]{1,0:T(8,128)(2,1)} %w_ref.1, bf16[512,256]{1,0:T(8,128)(2,1)} %og_ref.1, ...), custom_call_target="tpu_custom_call" | custom-call | tf_op jit(solution)/shard_map/graph_layer/pallas_call | solution.py:490
  70.3 2.2 %finish.1 = (bf16[512,256]{1,0:T(8,128)(2,1)}, f32[256,256]{1,0:T(8,128)}, f32[320,256]{1,0:T(8,128)}) custom-call(bf16[512,256]{1,0:T(8,128)(2,1)} %get-tuple-element.7.hid_in, f32[1,512]{1,0:T(1,128)} %get-tuple-element.8.rowr_in, bf16[16,2,16,256]{3,2,1,0:T(8,128)(2,1)} %get-tuple-element.9.gg_in, bf16[16,16,256]{2,1,0:T(8,128)(2,1)} %get-tuple-element.10.wd_in), custom_call_target="tpu_custom_call" | custom-call | tf_op jit(solution)/shard_map/finish/pallas_call | solution.py:558

commit v5 on v4

--- a/solution.py
+++ b/solution.py
@@ -68,12 +68,13 @@
     kw = r * 2 + h
     quad = lax.rem(b, 4)
     R1, R2, G, WA, WB, WC, WD, A2 = range(8)
-    XF, XB, A2S, SELF, F1 = 8, 10, 12, 14, 16
+    XF, XS, A2S, SELF, F1, XB = 8, 10, 12, 14, 16, 20
 
     def at_blk(t):
         return {"blk": t, "mp": lax.rem(h + t, 2)}
 
-    def in_group(d):
+    def in_group(n):
+        d = 8 + jnp.where(lax.rem(n, 2) == 0, -(n // 2), n // 2 + 1)
         t = lax.rem(k + d, 16)
         return t // 2, lax.rem(t, 2)
 
@@ -92,6 +93,10 @@
             src, dst = staged[i]
             pltpu.make_async_copy(src, dst, in_sem.at[i]).start()
 
+    def arrived(i):
+        src, dst = staged[i]
+        pltpu.make_async_copy(src, dst, in_sem.at[i]).wait()
+
     start(0, 3)
 
     barrier = pltpu.get_barrier_semaphore()
@@ -115,18 +120,6 @@
         return 0
 
     lax.fori_loop(1, 8, greet_rep, 0)
-
-    start(3, 7)
-
-    def arrived(i):
-        src, dst = staged[i]
-        pltpu.make_async_copy(src, dst, in_sem.at[i]).wait()
-
-    for p in range(2):
-        pltpu.make_async_copy(
-            adj_ref.at[m + 2 * p], vall[p].at[pl.ds(0, 5)], loc_sem.at[p]
-        ).start()
-        vall[p][10] = jnp.zeros((128, 128), BF)
 
     iota = functools.partial(lax.broadcasted_iota, jnp.int32)
     expand = (2 * (iota((256, 32), 0) // 16) + h == iota((256, 32), 1)).astype(BF)
@@ -150,10 +143,15 @@
     def owner_at(d):
         return lax.rem(2 * lax.rem(z + d, 16) + parity - 4 * r - m + 64, 32) // 2
 
+    def half(p, far):
+        i = far if p else 1 - far
+        return i, pl.ds(4 * i, 4)
+
     def deliver(far):
+        low, top = F1 + half(0, far)[0], F1 + 2 + half(1, far)[0]
+
         def one(n, _):
             up = 7 - n
-            low, top = F1 + 1 - far, F1 + 2 + far
             send(
                 outg.at[owner_at(up)],
                 fq.at[0, n],
@@ -172,8 +170,8 @@
 
         lax.fori_loop(*((0, 4) if far else (4, 7)), one, 0)
 
+    deliver(0)
     deliver(1)
-    deliver(0)
 
     send(tiles_ref, mp_tv, key_ss.at[0], key_rs.at[0], mp=1 - m)
     send(mask_ref, mp_mv, key_ss.at[1], key_rs.at[1], mp=1 - m)
@@ -191,6 +189,14 @@
     def first_z(t, j):
         return lax.rem(t // 2 + (9 if j < 2 else 0), 16)
 
+    start(3, 7)
+
+    for p in range(2):
+        pltpu.make_async_copy(
+            adj_ref.at[m + 2 * p], vall[p].at[pl.ds(0, 5)], loc_sem.at[p]
+        ).start()
+        vall[p][10] = jnp.zeros((128, 128), BF)
+
     held = dot(counts, mine)
     expand_r = (iota((512, 32), 0) // 16 == iota((512, 32), 1)).astype(BF)
     in_slot_r = lax.rem(iota((512, 16), 0), 16) == iota((512, 16), 1)
@@ -242,16 +248,15 @@
                 denset[p, col * 128:(col + 1) * 128, row * 128:(row + 1) * 128] = tile.T
 
     def others(p):
-        for q, to in ((p, 1 - m + 2 * p), (1 - p, 2 * p), (1 - p, 2 * p + 1)):
+        for q, to in ((p, 1 - m + 2 * p), (1 - p, 1 - m + 2 * p), (1 - p, m + 2 * p)):
             yield q, to, lax.rem(b - m - 2 * q + to + 32, 32)
 
-    for far in (1, 0):
+    for far in (0, 1):
         for p in range(2):
-            sem = F1 + 2 * p + (far if p else 1 - far)
-            drain(fq.at[p, pl.ds(0, 3 + far)], rs.at[sem])
+            drain(fq.at[p, pl.ds(0, 3 + far)], rs.at[F1 + 2 * p + half(p, far)[0]])
         for p in range(2):
             for q, to, t in others(p):
-                piece = pl.ds(4 * (far if q else 1 - far), 4)
+                piece = half(q, far)[1]
                 send(
                     fq.at[q, piece],
                     fr.at[p, m + 2 * q, piece],
@@ -281,7 +286,7 @@
         send(r1s.at[2 * tr + tm], r1r.at[k], ss.at[R1], rs.at[R1], rep=tr, mp=tm)
         return 0
 
-    lax.fori_loop(1, 16, scatter, 0)
+    lax.fori_loop(0, 15, scatter, 0)
     r1r[k] = r1s[k]
     transpose(0)
     drain(r1r.at[pl.ds(0, 15)], rs.at[R1])
@@ -295,7 +300,7 @@
         send(agg.at[k], agg.at[k], ss.at[R2], rs.at[R2], rep=tr, mp=tm)
         return 0
 
-    lax.fori_loop(1, 16, gather, 0)
+    lax.fori_loop(0, 15, gather, 0)
     transpose(1)
     arrived(5)
     arrived(6)
@@ -329,15 +334,20 @@
             pb[p, q, 0:16] = terms[:, q]
             pb[p, q, 16:24] = terms[0:8, q]
         xr[p, m + 2 * p] = pb[p, parity, pl.ds(first_z(b, 2 * p), 8)]
-    for p in range(2):
-        for q, to, t in others(p):
-            send(
-                pb.at[q, lax.rem(t, 2), pl.ds(first_z(t, 2 * p), 8)],
-                xr.at[p, m + 2 * q],
-                ss.at[XB + q],
-                rs.at[XB + p],
-                **at_blk(t),
-            )
+
+    def swap_back(far):
+        for p in range(2):
+            i, piece = half(p, far)
+            for q, to, t in others(p):
+                send(
+                    pb.at[q, lax.rem(t, 2), pl.ds(first_z(t, 2 * p) + 4 * i, 4)],
+                    xr.at[p, m + 2 * q, piece],
+                    ss.at[XS + far],
+                    rs.at[XB + 2 * p + i],
+                    **at_blk(t),
+                )
+
+    swap_back(1)
     pltpu.make_async_copy(hidv, hid_ref, out_sem.at[0]).start()
 
     drain(war.at[pl.ds(0, 3)], rs.at[WA])
@@ -347,37 +357,44 @@
     for e in range(1, 8):
         send(wb, wbr.at[eighth], ss.at[WB], rs.at[WB], blk=lax.rem(b + 4 * e, 32))
 
-    for p in range(2):
-        drain(xr.at[p, pl.ds(0, 3)], rs.at[XB + p])
-        total = xr[p, 0].astype(F32)
-        for i in range(1, 4):
-            total += xr[p, i].astype(F32)
-        mb[p] = total.astype(BF)
-        c = lax.rem(b - 4 * r - m - 2 * p + 64, 32)
-        home, slot = c // 4, lax.rem(c, 4) // 2
-
-        def back(n, _):
-            away = 7 - n
-            send(
-                mb.at[p, n if p == 0 else away],
-                ar.at[slot, r],
-                ss.at[A2S + p],
-                rs.at[A2],
-                blk=lax.rem(b + (32 - 2 * away if p == 0 else 2 * away), 32),
-                rep=home,
-            )
-            return 0
-
-        lax.fori_loop(0, 7, back, 0)
-        here = 7 if p == 0 else 0
-
-        @pl.when(home == r)
-        def _():
-            pltpu.make_async_copy(mb.at[p, here], ar.at[slot, r], rs.at[A2]).start()
-
-        @pl.when(home != r)
-        def _():
-            send(mb.at[p, here], ar.at[slot, r], ss.at[SELF + p], rs.at[A2], rep=home)
+    drain(xr.at[0, pl.ds(0, 3)], ss.at[XS + 1])
+    swap_back(0)
+
+    for far in (1, 0):
+        for p in range(2):
+            i, piece = half(p, far)
+            drain(xr.at[p, pl.ds(0, 3), piece], rs.at[XB + 2 * p + i])
+            total = xr[p, 0, piece].astype(F32)
+            for n in range(1, 4):
+                total += xr[p, n, piece].astype(F32)
+            mb[p, piece] = total.astype(BF)
+            c = lax.rem(b - 4 * r - m - 2 * p + 64, 32)
+            home, slot = c // 4, lax.rem(c, 4) // 2
+
+            def back(n, _):
+                away = 7 - n
+                send(
+                    mb.at[p, n if p == 0 else away],
+                    ar.at[slot, r],
+                    ss.at[A2S + p],
+                    rs.at[A2],
+                    blk=lax.rem(b + (32 - 2 * away if p == 0 else 2 * away), 32),
+                    rep=home,
+                )
+                return 0
+
+            lax.fori_loop(*((0, 4) if far else (4, 7)), back, 0)
+            if far:
+                continue
+            here = 7 if p == 0 else 0
+
+            @pl.when(home == r)
+            def _():
+                pltpu.make_async_copy(mb.at[p, here], ar.at[slot, r], rs.at[A2]).start()
+
+            @pl.when(home != r)
+            def _():
+                send(mb.at[p, here], ar.at[slot, r], ss.at[SELF + p], rs.at[A2], rep=home)
 
     drain(wbr.at[pl.ds(0, 7)], rs.at[WB])
     tile = wbr[0]
@@ -401,7 +418,22 @@
         send(wdv, wd_ref.at[kw], ss.at[WD], rs.at[WD], rep=tr, mp=tm)
         return 0
 
-    lax.fori_loop(1, 16, spread_w, 0)
+    lax.fori_loop(0, 15, spread_w, 0)
+
+    drain(mp_tv, key_ss.at[0])
+    drain(mp_mv, key_ss.at[1])
+    for p in range(2):
+        drain(vall[p].at[pl.ds(5, 5)], adj_ss.at[p])
+        for far in (0, 1):
+            drain(fq.at[p, pl.ds(0, 3 + far)], ss.at[F1 + 2 * p + half(p, far)[0]])
+        drain(fr.at[p, pl.ds(0, 3)], ss.at[XF + p])
+    drain(xr.at[0, pl.ds(0, 3)], ss.at[XS])
+    drain(r1r.at[pl.ds(0, 15)], ss.at[R1])
+    drain(agg.at[pl.ds(0, 15)], ss.at[R2])
+    drain(wa.at[pl.ds(0, 3)], ss.at[WA])
+    drain(wbr.at[pl.ds(0, 7)], ss.at[WB])
+    for i, (src, dst) in enumerate(((hidv, hid_ref), (rowrv, rowr_ref))):
+        pltpu.make_async_copy(src, dst, out_sem.at[i]).wait()
 
     drain(ar, rs.at[A2])
     total = ar[:, 0].astype(F32)
@@ -415,19 +447,12 @@
         send(gv, gg_ref.at[kw], ss.at[G], rs.at[G], rep=tr, mp=tm)
         return 0
 
-    lax.fori_loop(1, 16, share, 0)
+    lax.fori_loop(0, 15, share, 0)
 
     drain(wd_ref, rs.at[WD])
     drain(gg_ref, rs.at[G])
 
-    drain(mp_tv, key_ss.at[0])
-    drain(mp_mv, key_ss.at[1])
     for p in range(2):
-        drain(vall[p].at[pl.ds(5, 5)], adj_ss.at[p])
-        drain(fq.at[p, pl.ds(0, 4 if p == 0 else 3)], ss.at[F1 + 2 * p])
-        drain(fq.at[p, pl.ds(0, 3 if p == 0 else 4)], ss.at[F1 + 2 * p + 1])
-        drain(fr.at[p, pl.ds(0, 3)], ss.at[XF + p])
-        drain(xr.at[p, pl.ds(0, 3)], ss.at[XB + p])
         drain(mb.at[p, pl.ds(0, 7)], ss.at[A2S + p])
         c = lax.rem(b - 4 * r - m - 2 * p + 64, 32)
 
@@ -435,15 +460,9 @@
         def _():
             drain(mb.at[p, 0], ss.at[SELF + p])
 
-    drain(r1r.at[pl.ds(0, 15)], ss.at[R1])
-    drain(agg.at[pl.ds(0, 15)], ss.at[R2])
-    drain(gg_ref.at[pl.ds(0, 15)], ss.at[G])
-    drain(wa.at[pl.ds(0, 3)], ss.at[WA])
-    drain(wbr.at[pl.ds(0, 7)], ss.at[WB])
     drain(wc.at[pl.ds(0, 3)], ss.at[WC])
     drain(wd_ref.at[pl.ds(0, 15)], ss.at[WD])
-    for i, (src, dst) in enumerate(((hidv, hid_ref), (rowrv, rowr_ref))):
-        pltpu.make_async_copy(src, dst, out_sem.at[i]).wait()
+    drain(gg_ref.at[pl.ds(0, 15)], ss.at[G])
 
 
 def finish(hid_in, rowr_in, gg_in, wd_in, hid_ref, wg_ref, ig_ref, hid, rowr, gg, wd, wg, ig, sem):
@@ -538,8 +557,8 @@
             dma((2,)),
             dma((2,)),
             dma((2,)),
-            dma((20,)),
-            dma((20,)),
+            dma((24,)),
+            dma((24,)),
         ],
         compiler_params=pltpu.CompilerParams(
             collective_id=0, has_side_effects=True, vmem_limit_bytes=62 * 1024 * 1024

time: 72.7 us -> 69.3 us (0.953)
  Pallas kernels: 71.9 us -> 68.4 us
    pallas_call x1, Pallas kernels: 69.7 us -> 66.3 us  [shards(): pl.pallas_call(kernel, out_shape=between, in_specs=[hbm] * 8, out_specs=(...]
where the time goes in v5:
time: 69.3 us; the launch traced here: 69.1 us
  Pallas kernels  68.4 us (99%)
    pallas_call x1, Pallas kernels, shards(): pl.pallas_call(kernel, out_shape=between, in_specs=[hbm] * 8, out_specs=(...  66.3 us
    pallas_call x1, Pallas kernels, shards(): pl.pallas_call(finish, out_shape=outs, in_specs=[hbm] * 4, out_specs=(hbm...  2.16 us

profile of v5, /device:TPU:1, one launch (start us, length us, event | category | flops | bytes accessed | tf_op | source)
XLA Modules:
  0.0 69.1 jit_solution(1953896525221324608)
XLA Ops:
  0.6 66.3 %graph_layer.1 = (bf16[512,256]{1,0:T(8,128)(2,1)}, f32[1,512]{1,0:T(1,128)}, bf16[16,2,16,256]{3,2,1,0:T(8,128)(2,1)}, bf16[16,16,256]{2,1,0:T(8,128)(2,1)}) custom-call(s32[4,2,5]{2,1,0:T(2,128)} %bitcast.10, s32[4,5]{1,0:T(4,128)} %bitcast.11, bf16[320,256]{1,0:T(8,128)(2,1)} %x_ref.1, bf16[256,256]{1,0:T(8,128)(2,1)} %w_ref.1, bf16[512,256]{1,0:T(8,128)(2,1)} %og_ref.1, ...), custom_call_target="tpu_custom_call" | custom-call | tf_op jit(solution)/shard_map/graph_layer/pallas_call | solution.py:509
  66.9 2.2 %finish.1 = (bf16[512,256]{1,0:T(8,128)(2,1)}, f32[256,256]{1,0:T(8,128)}, f32[320,256]{1,0:T(8,128)}) custom-call(bf16[512,256]{1,0:T(8,128)(2,1)} %get-tuple-element.7.hid_in, f32[1,512]{1,0:T(1,128)} %get-tuple-element.8.rowr_in, bf16[16,2,16,256]{3,2,1,0:T(8,128)(2,1)} %get-tuple-element.9.gg_in, bf16[16,16,256]{2,1,0:T(8,128)(2,1)} %get-tuple-element.10.wd_in), custom_call_target="tpu_custom_call" | custom-call | tf_op jit(solution)/shard_map/finish/pallas_call | solution.py:577

commit v6 on v5

--- a/solution.py
+++ b/solution.py
@@ -335,12 +335,17 @@
             pb[p, q, 16:24] = terms[0:8, q]
         xr[p, m + 2 * p] = pb[p, parity, pl.ds(first_z(b, 2 * p), 8)]
 
+    def share_of(p, far):
+        i = half(p, far)[0]
+        first, count = ((5 if i else 0), 3) if far else ((3 if i else 0), 5)
+        return i, first, pl.ds(first, count)
+
     def swap_back(far):
         for p in range(2):
-            i, piece = half(p, far)
+            i, first, piece = share_of(p, far)
             for q, to, t in others(p):
                 send(
-                    pb.at[q, lax.rem(t, 2), pl.ds(first_z(t, 2 * p) + 4 * i, 4)],
+                    pb.at[q, lax.rem(t, 2), pl.ds(first_z(t, 2 * p) + first, piece.size)],
                     xr.at[p, m + 2 * q, piece],
                     ss.at[XS + far],
                     rs.at[XB + 2 * p + i],
@@ -357,12 +362,12 @@
     for e in range(1, 8):
         send(wb, wbr.at[eighth], ss.at[WB], rs.at[WB], blk=lax.rem(b + 4 * e, 32))
 
-    drain(xr.at[0, pl.ds(0, 3)], ss.at[XS + 1])
+    drain(xr.at[0, pl.ds(0, 3), pl.ds(0, 6)], ss.at[XS + 1])
     swap_back(0)
 
     for far in (1, 0):
         for p in range(2):
-            i, piece = half(p, far)
+            i, _, piece = share_of(p, far)
             drain(xr.at[p, pl.ds(0, 3), piece], rs.at[XB + 2 * p + i])
             total = xr[p, 0, piece].astype(F32)
             for n in range(1, 4):
@@ -383,7 +388,7 @@
                 )
                 return 0
 
-            lax.fori_loop(*((0, 4) if far else (4, 7)), back, 0)
+            lax.fori_loop(*((0, 3) if far else (3, 7)), back, 0)
             if far:
                 continue
             here = 7 if p == 0 else 0
@@ -427,7 +432,7 @@
         for far in (0, 1):
             drain(fq.at[p, pl.ds(0, 3 + far)], ss.at[F1 + 2 * p + half(p, far)[0]])
         drain(fr.at[p, pl.ds(0, 3)], ss.at[XF + p])
-    drain(xr.at[0, pl.ds(0, 3)], ss.at[XS])
+    drain(xr.at[pl.ds(0, 2), pl.ds(0, 3), pl.ds(0, 5)], ss.at[XS])
     drain(r1r.at[pl.ds(0, 15)], ss.at[R1])
     drain(agg.at[pl.ds(0, 15)], ss.at[R2])
     drain(wa.at[pl.ds(0, 3)], ss.at[WA])

time: 69.3 us -> 69 us (level)
  no operation moved by 1% of the time
where the time goes in v6:
time: 69 us; the launch traced here: 68.8 us
  Pallas kernels  68.2 us (99%)
    pallas_call x1, Pallas kernels, shards(): pl.pallas_call(kernel, out_shape=between, in_specs=[hbm] * 8, out_specs=(...  66 us
    pallas_call x1, Pallas kernels, shards(): pl.pallas_call(finish, out_shape=outs, in_specs=[hbm] * 4, out_specs=(hbm...  2.16 us

profile of v6, /device:TPU:1, one launch (start us, length us, event | category | flops | bytes accessed | tf_op | source)
XLA Modules:
  0.0 68.8 jit_solution(16285389118744198912)
XLA Ops:
  0.6 66.0 %graph_layer.1 = (bf16[512,256]{1,0:T(8,128)(2,1)}, f32[1,512]{1,0:T(1,128)}, bf16[16,2,16,256]{3,2,1,0:T(8,128)(2,1)}, bf16[16,16,256]{2,1,0:T(8,128)(2,1)}) custom-call(s32[4,2,5]{2,1,0:T(2,128)} %bitcast.10, s32[4,5]{1,0:T(4,128)} %bitcast.11, bf16[320,256]{1,0:T(8,128)(2,1)} %x_ref.1, bf16[256,256]{1,0:T(8,128)(2,1)} %w_ref.1, bf16[512,256]{1,0:T(8,128)(2,1)} %og_ref.1, ...), custom_call_target="tpu_custom_call" | custom-call | tf_op jit(solution)/shard_map/graph_layer/pallas_call | solution.py:514
  66.6 2.2 %finish.1 = (bf16[512,256]{1,0:T(8,128)(2,1)}, f32[256,256]{1,0:T(8,128)}, f32[320,256]{1,0:T(8,128)}) custom-call(bf16[512,256]{1,0:T(8,128)(2,1)} %get-tuple-element.7.hid_in, f32[1,512]{1,0:T(1,128)} %get-tuple-element.8.rowr_in, bf16[16,2,16,256]{3,2,1,0:T(8,128)(2,1)} %get-tuple-element.9.gg_in, bf16[16,16,256]{2,1,0:T(8,128)(2,1)} %get-tuple-element.10.wd_in), custom_call_target="tpu_custom_call" | custom-call | tf_op jit(solution)/shard_map/finish/pallas_call | solution.py:582

commit v7 on v6

--- a/solution.py
+++ b/solution.py
@@ -482,14 +482,14 @@
 
     arrived(0)
     place = (rowr[...] == lax.broadcasted_iota(jnp.int32, (320, 512), 0).astype(F32)).astype(BF)
+    arrived(3)
+    pltpu.make_async_copy(*outgoing[2], sem.at[6]).start()
     arrived(1)
     ig[...] = dot(place, gg[...].reshape(512, 256))
     pltpu.make_async_copy(*outgoing[0], sem.at[4]).start()
     arrived(2)
     wg[...] = wd[...].reshape(256, 256).astype(F32) * (1.0 / 128.0)
     pltpu.make_async_copy(*outgoing[1], sem.at[5]).start()
-    arrived(3)
-    pltpu.make_async_copy(*outgoing[2], sem.at[6]).start()
     for i, (src, dst) in enumerate(outgoing):
         pltpu.make_async_copy(src, dst, sem.at[4 + i]).wait()
 

time: 69 us -> 69.1 us (level)
  no operation moved by 1% of the time
where the time goes in v7:
time: 69.1 us; the launch traced here: 68.9 us
  Pallas kernels  68.2 us (99%)
    pallas_call x1, Pallas kernels, shards(): pl.pallas_call(kernel, out_shape=between, in_specs=[hbm] * 8, out_specs=(...  66 us
    pallas_call x1, Pallas kernels, shards(): pl.pallas_call(finish, out_shape=outs, in_specs=[hbm] * 4, out_specs=(hbm...  2.22 us

profile of v7, /device:TPU:1, one launch (start us, length us, event | category | flops | bytes accessed | tf_op | source)
XLA Modules:
  0.0 68.9 jit_solution(14128958622288288649)
XLA Ops:
  0.6 66.0 %graph_layer.1 = (bf16[512,256]{1,0:T(8,128)(2,1)}, f32[1,512]{1,0:T(1,128)}, bf16[16,2,16,256]{3,2,1,0:T(8,128)(2,1)}, bf16[16,16,256]{2,1,0:T(8,128)(2,1)}) custom-call(s32[4,2,5]{2,1,0:T(2,128)} %bitcast.10, s32[4,5]{1,0:T(4,128)} %bitcast.11, bf16[320,256]{1,0:T(8,128)(2,1)} %x_ref.1, bf16[256,256]{1,0:T(8,128)(2,1)} %w_ref.1, bf16[512,256]{1,0:T(8,128)(2,1)} %og_ref.1, ...), custom_call_target="tpu_custom_call" | custom-call | tf_op jit(solution)/shard_map/graph_layer/pallas_call | solution.py:514
  66.6 2.2 %finish.1 = (bf16[512,256]{1,0:T(8,128)(2,1)}, f32[256,256]{1,0:T(8,128)}, f32[320,256]{1,0:T(8,128)}) custom-call(bf16[512,256]{1,0:T(8,128)(2,1)} %get-tuple-element.7.hid_in, f32[1,512]{1,0:T(1,128)} %get-tuple-element.8.rowr_in, bf16[16,2,16,256]{3,2,1,0:T(8,128)(2,1)} %get-tuple-element.9.gg_in, bf16[16,16,256]{2,1,0:T(8,128)(2,1)} %get-tuple-element.10.wd_in), custom_call_target="tpu_custom_call" | custom-call | tf_op jit(solution)/shard_map/finish/pallas_call | solution.py:582
